TPU v7x, 32 devices: a whole 2x2x4 slice. The times are simulated.
32 devices in a mesh: seq: 4 (over z), section: 2 (over core), batch: 4 (over y, x).
Axes of the slice: x: 2, y: 2, z: 4, core: 2. Of those that a mesh axis runs over, the one named last changes fastest.
Arguments:
- features: bfloat16 [4, 16384, 768], P('batch', 'seq'), may hold values from -6 to 6
- dilated_tap_weight: bfloat16 [3, 768, 768], P(None, None, 'section'), may hold values from -0.125 to 0.125
- strided_weight: bfloat16 [2, 768, 1536], P(None, None, 'section'), may hold values from -0.15625 to 0.15625
- norm_gain: float32 [1536], replicated, may hold values from 0.1 to 1.9
- query_weight: bfloat16 [1536, 1024], P(None, 'section'), may hold values from -0.15625 to 0.15625
- key_weight: bfloat16 [1536, 1024], P(None, 'section'), may hold values from -0.15625 to 0.15625
- value_weight: bfloat16 [1536, 1536], P(None, 'section'), may hold values from -0.15625 to 0.15625
- output_weight: bfloat16 [1536, 1536], P('section'), may hold values from -0.15625 to 0.15625
- position_bias: float32 [4, 8, 128, 128], P('batch', 'section', 'seq'), may hold values from -4 to 320
- interval_start: int32 [4, 128], P('batch', 'seq'), may hold values from 0 to 126, as said below
- interval_end: int32 [4, 128], P('batch', 'seq'), may hold values from 2 to 128, as said below
- cotangent: bfloat16 [4, 128, 1536], P('batch', 'seq'), may hold values from -0.19921875 to 0.19921875
Outputs:
- layer_out: bfloat16 [4, 128, 1536], P('batch', 'seq', 'section')
- output_grad: float32 [1536, 1536], P('section')
Inputs may be any that keep to these rules, and one draw needn't show every extreme that they name: interval_start[b, i] <= max(i - 1, 0): each query sees itself and the position before it. interval_end[b, i] >= min(i + 2, 128): each query sees the position after it.
All inputs are finite; a program needn't handle non-finite values.
Results may differ from a plain program's by a relative error of at most 0.02.
Values may be sent and summed in bfloat16 or wider, within the bound.
A program may use at most 128 MiB of HBM per device.

v0:
```python
import jax
import jax.numpy as jnp
from jax import lax
from jax.sharding import PartitionSpec as P

KEY = 128
VAL = 192
POOL = 128
DILATION_STEP = 8


def padded(shard, sides, width):
    for axis, dim in sides:
        size, length = (lax.axis_size(axis), shard.shape[dim])
        up = [(i, (i + 1) % size) for i in range(size - 1)]
        down = [(j, i) for i, j in up]
        last = lax.slice_in_dim(shard, length - width, length, axis=dim)
        leading = lax.slice_in_dim(shard, 0, width, axis=dim)
        before = lax.ppermute(last, axis, up)
        after = lax.ppermute(leading, axis, down)
        shard = jnp.concatenate([before, shard, after], axis=dim)
    return shard


def dilated_block(padded_input, local_sequence, weight_arrays, begin):
    sequence_length = local_sequence.shape[0]
    columns = weight_arrays.shape[2]
    before_activation = jnp.dot(
        padded_input[0:sequence_length], weight_arrays[0], preferred_element_type=jnp.float32
    )
    before_activation = before_activation + jnp.dot(
        padded_input[DILATION_STEP : DILATION_STEP + sequence_length],
        weight_arrays[1],
        preferred_element_type=jnp.float32,
    )
    before_activation = before_activation + jnp.dot(
        padded_input[2 * DILATION_STEP : 2 * DILATION_STEP + sequence_length],
        weight_arrays[2],
        preferred_element_type=jnp.float32,
    )
    own_cols = lax.dynamic_slice_in_dim(local_sequence, begin, columns, 1)
    return (own_cols.astype(jnp.float32) + jax.nn.gelu(before_activation)).astype(jnp.bfloat16)


def shards(
    features,
    dilated_tap_weight,
    strided_weight,
    norm_gain,
    query_weight,
    key_weight,
    value_weight,
    output_weight,
    position_bias,
    interval_start,
    interval_end,
    cotangent,
):
    local_sequence = features[0]
    sequence_length = local_sequence.shape[0]
    padded_input = padded(local_sequence, (("seq", 0),), DILATION_STEP)
    out_cols = strided_weight.shape[2]
    hidden = dilated_block(
        padded_input,
        local_sequence,
        dilated_tap_weight,
        lax.axis_index("section") * dilated_tap_weight.shape[2],
    )
    piece = lax.all_gather(hidden, "section", axis=1, tiled=True)
    width = piece.shape[1]
    paired = piece.reshape(sequence_length // 2, 2 * width)
    taps = strided_weight.reshape(2 * width, out_cols)
    strided = jnp.dot(paired, taps, preferred_element_type=jnp.float32)
    pooled = (
        strided.reshape(sequence_length // POOL, POOL // 2, out_cols)
        .max(axis=1)
        .astype(jnp.bfloat16)
    )
    gathered = lax.all_gather(pooled, "section", axis=1, tiled=True)
    values_f = gathered.astype(jnp.float32)
    centred = values_f - jnp.mean(values_f, axis=1, keepdims=True)
    spread = jnp.mean(centred * centred, axis=1, keepdims=True)
    normed = centred * lax.rsqrt(spread + 1e-05) * norm_gain
    inputs_b = normed.astype(jnp.bfloat16)
    query = (
        jnp.dot(inputs_b, query_weight, preferred_element_type=jnp.float32) * KEY ** (-0.5)
    ).astype(jnp.bfloat16)
    keyed = jnp.dot(inputs_b, key_weight, preferred_element_type=jnp.float32).astype(jnp.bfloat16)
    valued = jnp.dot(inputs_b, value_weight, preferred_element_type=jnp.float32).astype(
        jnp.bfloat16
    )
    rows = query.shape[0]
    heads_local = query.shape[1] // KEY
    query3 = query.reshape(rows, heads_local, KEY)
    bias_local = position_bias[0]
    lower = interval_start[0]
    upper = interval_end[0]
    best = jnp.full((heads_local, rows), -1e30, jnp.float32)
    key_piece = lax.all_gather(keyed, "seq", axis=0, tiled=True)
    value_piece = lax.all_gather(valued, "seq", axis=0, tiled=True)
    count = key_piece.shape[0]
    key3 = key_piece.reshape(count, heads_local, KEY)
    value3 = value_piece.reshape(count, heads_local, VAL)
    scores = jnp.einsum("qhd,khd->hqk", query3, key3, preferred_element_type=jnp.float32)
    scores = scores + bias_local
    positions = jnp.arange(count, dtype=jnp.int32)
    visible = (positions[None, :] >= lower[:, None]) & (positions[None, :] < upper[:, None])
    scores = jnp.where(visible[None], scores, jnp.float32(-1e30))
    newest = jnp.maximum(best, jnp.max(scores, axis=2))
    weight_arrays = jnp.where(visible[None], jnp.exp(scores - newest[:, :, None]), jnp.float32(0.0))
    weight_sum = jnp.sum(weight_arrays, axis=2)
    accum = jnp.einsum(
        "hqk,khd->hqd",
        weight_arrays.astype(jnp.bfloat16),
        value3,
        preferred_element_type=jnp.float32,
    )
    final_best, weight_sum, accum = (newest, weight_sum, accum)
    attended = (
        (accum / weight_sum[:, :, None])
        .transpose(1, 0, 2)
        .reshape(rows, heads_local * VAL)
        .astype(jnp.bfloat16)
    )
    projected = jnp.dot(attended, output_weight, preferred_element_type=jnp.float32)
    mixed = lax.psum_scatter(projected, "section", scatter_dimension=1, tiled=True)
    own_norm = lax.dynamic_slice_in_dim(normed, lax.axis_index("section") * out_cols, out_cols, 1)
    layer_out = (own_norm + mixed).astype(jnp.bfloat16)[None]
    grad_term = jnp.dot(attended.T, cotangent[0], preferred_element_type=jnp.float32)
    output_grad = lax.psum(grad_term, ("seq", "batch"))
    return (layer_out, output_grad)


def solution(mesh):
    return jax.shard_map(
        shards,
        mesh=mesh,
        in_specs=(
            P("batch", "seq", None),
            P(None, None, "section"),
            P(None, None, "section"),
            P(),
            P(None, "section"),
            P(None, "section"),
            P(None, "section"),
            P("section", None),
            P("batch", "section", "seq", None),
            P("batch", "seq"),
            P("batch", "seq"),
            P("batch", "seq", None),
        ),
        out_specs=(P("batch", "seq", "section"), P("section", None)),
        check_vma=False,
    )
```

profile of v0, /device:TPU:0, one launch (start us, length us, event | category | flops | bytes accessed | tf_op | source)
XLA Modules:
  0.0 318.1 jit_solution(5371152659783682737)
XLA Ops:
  7.2 0.0 copy-start
  7.2 0.0 all-gather.2.cloned.1.call-start
  7.2 0.9 slice_bitcast_fusion
  8.1 4.9 %collective-permute-start = (bf16[8,768]{1,0:T(8,128)(2,1)S(1)}, bf16[8,768]{1,0:T(8,128)(2,1)S(1)}, u32[]{:S(2)}, u32[]{:S(2)}) collective-permute-start(bf16[8,768]{1,0:T(8,128)(2,1)S(1)} %get-tuple-element.3), channel_id=1, source_target_pairs={{0,8},{8,16},{16,24},{1,9},{9,17},{17,25},{2,10},{10,18},{18,26},{... | collective-permute-start | bytes 36872 | tf_op jit(solution)/shard_map/ppermute | solution.py:19
  13.0 1.3 collective-permute-start.1
  14.3 9.0 %fusion.21 = f32[4096,384]{1,0:T(8,128)} fusion(bf16[3,768,384]{2,1,0:T(8,128)(2,1)} %param.13, bf16[1,4096,768]{2,1,0:T(8,128)(2,1)} %param.12), kind=kOutput, calls=%fused_computation.28 | convolution fusion | flops 2415919104 | bytes 13172736 | tf_op jit(solution)/shard_map/dot_general | solution.py:31
  23.3 0.0 collective-permute-done
  23.3 0.0 copy-start.9
  23.3 0.0 copy-start.10
  23.3 6.4 %fusion.11 = f32[4096,384]{1,0:T(8,128)S(1)} fusion(bf16[4096,768]{1,0:T(8,128)(2,1)} %bitcast.71, bf16[8,768]{1,0:T(8,128)(2,1)S(1)} %collective-permute-done, bf16[3,768,384]{2,1,0:T(8,128)(2,1)} %param.13), kind=kOutput, calls=%fused_computation.14 | convolution fusion | flops 2428502016 | bytes 13185024 | tf_op jit(solution)/shard_map/dot_general | solution.py:28
  29.7 0.0 copy-start.7
  29.7 0.0 copy-start.8
  29.8 0.0 collective-permute-done.1
  29.8 0.0 copy-done.9
  29.8 0.1 copy-done.10
  29.9 8.3 %fusion.8 = bf16[4096,384]{1,0:T(8,128)(2,1)} fusion(f32[4096,384]{1,0:T(8,128)S(1)} %fusion.11, f32[4096,384]{1,0:T(8,128)S(1)} %copy-done.10, bf16[1,4096,768]{2,1,0:T(8,128)(2,1)S(1)} %copy-done.9, s32[]{:T(128)S(6)} %select_n.13, bf16[8,768]{1,0:T(8,128)(2,1)S(1)} %collective-permute-done.1, bf16[4096,768]{1,0:T(8,128)(2,1)S(1)} %bitcast.72, ...), kind=kOutput, calls=%fused_computation.9 | convolution fusion | flops 2448949248 | bytes 25767940 | tf_op jit(solution)/shard_map/dot_general | solution.py:36
  38.2 0.0 all-gather.2.cloned.1.call-update
  38.2 0.0 reduce-scatter.2.cloned.1.call-start
  38.2 0.0 copy-done.7
  38.3 0.0 copy-done.8
  38.3 0.1 fusion.44
  38.3 18.9 %all-gather.2.cloned.1.call-done = bf16[4096,768]{1,0:T(8,128)(2,1)} async-done(((bf16[4096,384]{1,0:T(8,128)(2,1)}), bf16[4096,768]{1,0:T(8,128)(2,1)}) %all-gather.2.cloned.1.call-update) | async-done | bytes 6291472 | tf_op jit(solution)/shard_map/all_gather | solution.py:69
  57.2 10.0 %dot_general.40 = bf16[32,64,1536]{2,1,0:T(8,128)(2,1)} reshape(bf16[4096,768]{1,0:T(8,128)(2,1)} %all-gather.2.cloned.1.call-done) | data formatting | bytes 12582912 | tf_op jit(solution)/shard_map/dot_general | solution.py:73
  67.3 0.0 copy-done
  67.3 0.0 copy-start.2
  67.3 0.0 copy-start.4
  67.3 0.0 copy-start.3
  67.3 0.0 copy-start.6
  67.3 0.0 copy-start.1
  67.3 8.4 %convolution_reduce_fusion = bf16[32,768]{1,0:T(8,128)(2,1)S(1)} fusion(bf16[32,64,1536]{2,1,0:T(8,128)(2,1)} %dot_general.40, bf16[1536,768,1]{1,0,2:T(8,128)(2,1)S(1)} %bitcast.66), kind=kOutput, calls=%fused_computation.16 | convolution fusion | flops 4833386496 | bytes 8699904 | tf_op jit(solution)/shard_map/dot_general | solution.py:73
  75.7 0.0 copy-start.5
  75.7 2.0 all_gather.13
  77.7 0.1 convert_reduce_fusion
  77.9 0.2 fusion.29
  78.1 0.0 copy-done.2
  78.1 0.0 copy-done.4
  78.1 0.4 convolution_convert_fusion.1
  78.5 13.7 %all_gather.14 = bf16[128,512]{1,0:T(8,128)(2,1)S(1)} all-gather(bf16[32,512]{1,0:T(8,128)(2,1)S(1)} %convolution_convert_fusion.1), channel_id=1, replica_groups=mesh['seq'=4,'section'=2,'batch'=4] {'seq'}, dimensions={0}, use_global_device_ids=true | all-gather | bytes 163840 | tf_op jit(solution)/shard_map/all_gather | solution.py:99
  92.3 0.0 copy-done.3
  92.3 0.4 fusion.17
  92.7 0.0 copy-done.6
  92.7 0.2 fusion.55
  93.0 0.0 copy-done.1
  93.0 0.6 convolution_convert_fusion
  93.5 13.9 %all_gather.15 = bf16[128,768]{1,0:T(8,128)(2,1)S(1)} all-gather(bf16[32,768]{1,0:T(8,128)(2,1)S(1)} %convolution_convert_fusion), channel_id=1, replica_groups=mesh['seq'=4,'section'=2,'batch'=4] {'seq'}, dimensions={0}, use_global_device_ids=true | all-gather | bytes 245760 | tf_op jit(solution)/shard_map/all_gather | solution.py:100
  107.4 0.2 copy.19
  107.6 0.2 fusion.35
  107.8 0.2 fusion.14
  108.0 0.1 copy.20
  108.1 0.1 convert_element_type.51
  108.2 2.8 fusion.56
  111.1 0.0 reduce-scatter.2.cloned.1.call-update
  111.1 0.0 all-reduce.2.cloned.1.call-start
  111.1 0.0 copy-done.5
  111.1 3.0 fusion.33
  114.1 0.0 all-reduce.2.cloned.1.call-update
  114.2 0.1 fusion.30
  114.3 5.3 %reduce-scatter.2.cloned.1.call-done = f32[32,768]{1,0:T(8,128)} async-done(((f32[32,1536]{1,0:T(8,128)}), f32[32,768]{1,0:T(8,128)}) %reduce-scatter.2.cloned.1.call-update) | async-done | bytes 98320 | tf_op jit(solution)/shard_map/reduce_scatter | solution.py:126
  119.5 1.5 fusion.37
  121.1 185.7 %all-reduce.2.cloned.1.call-done = f32[768,1536]{1,0:T(8,128)} async-done(((f32[768,1536]{1,0:T(8,128)}), f32[768,1536]{1,0:T(8,128)}) %all-reduce.2.cloned.1.call-update) | async-done | bytes 4718608 | tf_op jit(solution)/shard_map/psum | solution.py:130
  306.7 4.8 %copy.36 = f32[768,1536]{1,0:T(8,128)} copy(f32[768,1536]{1,0:T(8,128)} %all-reduce.2.cloned.1.call-done) | data formatting | bytes 9437184
  (3 shorter events, 0.0 us)
Async XLA Ops:
  7.2 60.1 %copy-start = (bf16[2,768,768]{2,1,0:T(8,128)(2,1)S(1)}, bf16[2,768,768]{2,1,0:T(8,128)(2,1)}, u32[]{:S(2)}) copy-start(bf16[2,768,768]{2,1,0:T(8,128)(2,1)} %param.14) | copy-start | bytes 7077892
  7.2 50.1 %all-gather.2.cloned.1.call-start = ((), (), s32[]{:S(2)}) async-start(), calls=%async_computation.1 | async-start | bytes 9437184 | tf_op jit(solution)/shard_map/all_gather | solution.py:69
  8.1 15.2 %collective-permute-start = (bf16[8,768]{1,0:T(8,128)(2,1)S(1)}, bf16[8,768]{1,0:T(8,128)(2,1)S(1)}, u32[]{:S(2)}, u32[]{:S(2)}) collective-permute-start(bf16[8,768]{1,0:T(8,128)(2,1)S(1)} %get-tuple-element.3), channel_id=1, source_target_pairs={{0,8},{8,16},{16,24},{1,9},{9,17},{17,25},{2,10},{10,18},{18,26},{... | collective-permute-start | bytes 36872 | tf_op jit(solution)/shard_map/ppermute | solution.py:19
  13.0 16.7 %collective-permute-start.1 = (bf16[8,768]{1,0:T(8,128)(2,1)S(1)}, bf16[8,768]{1,0:T(8,128)(2,1)S(1)}, u32[]{:S(2)}, u32[]{:S(2)}) collective-permute-start(bf16[8,768]{1,0:T(8,128)(2,1)S(1)} %get-tuple-element.2), channel_id=1, source_target_pairs={{8,0},{16,8},{24,16},{9,1},{17,9},{25,17},{10,2},{18,10},{26,18},{... | collective-permute-start | bytes 36872 | tf_op jit(solution)/shard_map/ppermute | solution.py:20
  23.3 6.5 %copy-start.9 = (bf16[1,4096,768]{2,1,0:T(8,128)(2,1)S(1)}, bf16[1,4096,768]{2,1,0:T(8,128)(2,1)}, u32[]{:S(2)}) copy-start(bf16[1,4096,768]{2,1,0:T(8,128)(2,1)} %param.12) | copy-start | bytes 18874372
  23.3 6.6 %copy-start.10 = (f32[4096,384]{1,0:T(8,128)S(1)}, f32[4096,384]{1,0:T(8,128)}, u32[]{:S(2)}) copy-start(f32[4096,384]{1,0:T(8,128)} %fusion.21) | copy-start | bytes 18874372
  29.7 8.5 %copy-start.7 = (s32[1,32]{1,0:T(1,128)S(1)}, s32[1,32]{1,0:T(1,128)}, u32[]{:S(2)}) copy-start(s32[1,32]{1,0:T(1,128)} %param.22) | copy-start | bytes 388
  29.7 8.5 %copy-start.8 = (s32[1,32]{1,0:T(1,128)S(1)}, s32[1,32]{1,0:T(1,128)}, u32[]{:S(2)}) copy-start(s32[1,32]{1,0:T(1,128)} %param.21) | copy-start | bytes 388
  38.2 81.3 %reduce-scatter.2.cloned.1.call-start = ((), (), s32[]{:S(2)}) async-start(), calls=%async_computation.2 | async-start | bytes 294912 | tf_op jit(solution)/shard_map/reduce_scatter | solution.py:126
  67.3 10.8 %copy-start.2 = (bf16[1536,512]{1,0:T(8,128)(2,1)S(1)}, bf16[1536,512]{1,0:T(8,128)(2,1)}, u32[]{:S(2)}) copy-start(bf16[1536,512]{1,0:T(8,128)(2,1)} %param.17) | copy-start | bytes 4718596
  67.3 10.8 %copy-start.4 = (f32[1536]{0:T(1024)S(1)}, f32[1536]{0:T(1024)}, u32[]{:S(2)}) copy-start(f32[1536]{0:T(1024)} %param.15) | copy-start | bytes 18436
  67.3 25.0 %copy-start.3 = (bf16[1536,512]{1,0:T(8,128)(2,1)S(1)}, bf16[1536,512]{1,0:T(8,128)(2,1)}, u32[]{:S(2)}) copy-start(bf16[1536,512]{1,0:T(8,128)(2,1)} %param.16) | copy-start | bytes 4718596
  67.3 25.4 %copy-start.6 = (f32[1,4,32,128]{3,2,1,0:T(8,128)S(1)}, f32[1,4,32,128]{3,2,1,0:T(8,128)}, u32[]{:S(2)}) copy-start(f32[1,4,32,128]{3,2,1,0:T(8,128)} %param.20) | copy-start | bytes 196612
  67.3 25.7 %copy-start.1 = (bf16[1536,768]{1,0:T(8,128)(2,1)S(1)}, bf16[1536,768]{1,0:T(8,128)(2,1)}, u32[]{:S(2)}) copy-start(bf16[1536,768]{1,0:T(8,128)(2,1)} %param.18) | copy-start | bytes 7077892
  75.7 35.4 %copy-start.5 = (bf16[1,32,1536]{2,1,0:T(8,128)(2,1)S(1)}, bf16[1,32,1536]{2,1,0:T(8,128)(2,1)}, u32[]{:S(2)}) copy-start(bf16[1,32,1536]{2,1,0:T(8,128)(2,1)} %param.23) | copy-start | bytes 294916
  111.1 195.6 %all-reduce.2.cloned.1.call-start = ((), (), s32[]{:S(2)}) async-start(), calls=%async_computation.3 | async-start | bytes 9437184 | tf_op jit(solution)/shard_map/psum | solution.py:130
Sparse Core Ops, SparseCore 0:
  38.3 18.8 all-gather.1
  111.2 8.2 reduce-scatter.1
  125.9 180.8 all-reduce.1
where the time goes:
time: 319 us; the launch traced here: 318 us
  waiting for transfers between devices  210 us (66%)
  matrix products  39.7 us (12%)
  blocking collectives  29.7 us (9%)
  local copies, waits for them, and re-layouts  16.3 us (5%)
  between operations  14 us (4%)
  starting transfers between devices  6.33 us (2%)
    psum x1, waiting for transfers between devices, shards(): output_grad = lax.psum(grad_term, ('seq', 'batch'))  186 us
    all_gather x1, waiting for transfers between devices, shards(): piece = lax.all_gather(hidden, 'section', axis=1, tiled=True)  18.9 us
    all_gather x1, blocking collectives, shards(): value_piece = lax.all_gather(valued, 'seq', axis=0, tiled=True)  13.9 us
    all_gather x1, blocking collectives, shards(): key_piece = lax.all_gather(keyed, 'seq', axis=0, tiled=True)  13.7 us
    dot_general x1, local copies, waits for them, and re-layouts, shards(): strided = jnp.dot(paired, taps, preferred_element_type=jnp.float32)  10 us
    dot_general x1, matrix products, dilated_block(): jnp.dot(padded_input[DILATION_STEP:DILATION_STEP + sequence_length], weig...  8.95 us
    dot_general x1, matrix products, shards(): strided = jnp.dot(paired, taps, preferred_element_type=jnp.float32)  8.39 us
    dot_general x1, matrix products, dilated_block(): jnp.dot(padded_input[2 * DILATION_STEP:2 * DILATION_STEP + sequence_lengt...  8.26 us
  transfers between devices with their start and end apart: 5, of which 3 were waited for; matrix products, arithmetic and copies ran while one was open for 6% of the time, Pallas kernels for 0%

commit v1 on v0

--- a/solution.py
+++ b/solution.py
@@ -56,6 +56,7 @@
     interval_end,
     cotangent,
 ):
+    cotangent_all = lax.all_gather(cotangent[0], ("batch", "seq"), axis=0, tiled=True)
     local_sequence = features[0]
     sequence_length = local_sequence.shape[0]
     padded_input = padded(local_sequence, (("seq", 0),), DILATION_STEP)
@@ -126,8 +127,13 @@
     mixed = lax.psum_scatter(projected, "section", scatter_dimension=1, tiled=True)
     own_norm = lax.dynamic_slice_in_dim(normed, lax.axis_index("section") * out_cols, out_cols, 1)
     layer_out = (own_norm + mixed).astype(jnp.bfloat16)[None]
-    grad_term = jnp.dot(attended.T, cotangent[0], preferred_element_type=jnp.float32)
-    output_grad = lax.psum(grad_term, ("seq", "batch"))
+    attended_all = lax.all_gather(attended, ("batch", "seq"), axis=0, tiled=True)
+    output_grad = lax.dot_general(
+        attended_all,
+        cotangent_all,
+        (((0,), (0,)), ((), ())),
+        preferred_element_type=jnp.float32,
+    )
     return (layer_out, output_grad)
 
 

time: 319 us -> 177 us (0.55)
  waiting for transfers between devices: 210 us -> 19 us
  blocking collectives: 29.7 us -> 79 us
  matrix products: 39.7 us -> 44.7 us
  local copies, waits for them, and re-layouts: 16.3 us -> 11.4 us
    psum x1 -> x0, waiting for transfers between devices: 186 us -> none  [shards(): output_grad = lax.psum(grad_term, ('seq', 'batch'))]
    all_gather x0 -> x1, blocking collectives: none -> 48.8 us  [shards(): lax.all_gather(attended, ('batch', 'seq'), axis=0, tiled=True)]
    reduce_scatter x1, waiting for transfers between devices: 5.29 us -> 0.01 us  [shards(): lax.psum_scatter(projected, 'section', scatter_dimension=1, tiled=True)]
    unnamed x23 -> x16, local copies, waits for them, and re-layouts: 5.04 us -> 0.18 us
  transfers between devices with their start and end apart: 5 -> 5, of which waited for: 3 -> 1; matrix products, arithmetic and copies ran while one was open for 6% -> 27% of each run, Pallas kernels for 0% -> 0%
where the time goes in v1:
time: 177 us
  blocking collectives  79 us (45%)
  matrix products  44.7 us (25%)
  waiting for transfers between devices  19 us (11%)
  between operations  14 us (8%)
  local copies, waits for them, and re-layouts  11.4 us (6%)
  starting transfers between devices  6.33 us (4%)
  other arithmetic  2.22 us (1%)
    all_gather x1, blocking collectives, shards(): lax.all_gather(attended, ('batch', 'seq'), axis=0, tiled=True)  48.8 us
    all_gather x1, waiting for transfers between devices, shards(): piece = lax.all_gather(hidden, 'section', axis=1, tiled=True)  18.2 us
    all_gather x1, blocking collectives, shards(): value_piece = lax.all_gather(valued, 'seq', axis=0, tiled=True)  14.6 us
    all_gather x1, blocking collectives, shards(): key_piece = lax.all_gather(keyed, 'seq', axis=0, tiled=True)  13.7 us
    dot_general x1, local copies, waits for them, and re-layouts, shards(): strided = jnp.dot(paired, taps, preferred_element_type=jnp.float32)  10 us
    dot_general x1, matrix products, dilated_block(): jnp.dot(padded_input[DILATION_STEP:DILATION_STEP + sequence_length], weig...  8.95 us
    dot_general x1, matrix products, shards(): strided = jnp.dot(paired, taps, preferred_element_type=jnp.float32)  8.47 us
    dot_general x1, matrix products, dilated_block(): jnp.dot(padded_input[2 * DILATION_STEP:2 * DILATION_STEP + sequence_lengt...  8.26 us
  transfers between devices with their start and end apart: 5, of which 1 were waited for; matrix products, arithmetic and copies ran while one was open for 27% of the time, Pallas kernels for 0%

profile of v1, /device:TPU:0, one launch (start us, length us, event | category | flops | bytes accessed | tf_op | source)
XLA Modules:
  0.0 176.5 jit_solution(4388175668013153202)
XLA Ops:
  7.2 0.0 copy-start
  7.2 0.0 all-gather.4.cloned.1.call-start
  7.2 0.9 slice_bitcast_fusion
  8.1 4.9 %collective-permute-start = (bf16[8,768]{1,0:T(8,128)(2,1)S(1)}, bf16[8,768]{1,0:T(8,128)(2,1)S(1)}, u32[]{:S(2)}, u32[]{:S(2)}) collective-permute-start(bf16[8,768]{1,0:T(8,128)(2,1)S(1)} %get-tuple-element.3), channel_id=1, source_target_pairs={{0,8},{8,16},{16,24},{1,9},{9,17},{17,25},{2,10},{10,18},{18,26},{... | collective-permute-start | bytes 36872 | tf_op jit(solution)/shard_map/ppermute | solution.py:19
  13.0 1.3 collective-permute-start.1
  14.3 9.0 %fusion.23 = f32[4096,384]{1,0:T(8,128)} fusion(bf16[3,768,384]{2,1,0:T(8,128)(2,1)} %param.13, bf16[1,4096,768]{2,1,0:T(8,128)(2,1)} %param.12), kind=kOutput, calls=%fused_computation.30 | convolution fusion | flops 2415919104 | bytes 13172736 | tf_op jit(solution)/shard_map/dot_general | solution.py:31
  23.3 0.0 collective-permute-done
  23.3 0.0 copy-start.6
  23.3 0.0 copy-start.7
  23.3 6.4 %fusion.11 = f32[4096,384]{1,0:T(8,128)S(1)} fusion(bf16[4096,768]{1,0:T(8,128)(2,1)} %bitcast.71, bf16[8,768]{1,0:T(8,128)(2,1)S(1)} %collective-permute-done, bf16[3,768,384]{2,1,0:T(8,128)(2,1)} %param.13), kind=kOutput, calls=%fused_computation.14 | convolution fusion | flops 2428502016 | bytes 13185024 | tf_op jit(solution)/shard_map/dot_general | solution.py:28
  29.7 0.0 copy-start.4
  29.7 0.0 copy-start.5
  29.8 0.0 collective-permute-done.1
  29.8 0.0 copy-done.6
  29.8 0.1 copy-done.7
  29.9 8.3 %fusion.8 = bf16[4096,384]{1,0:T(8,128)(2,1)} fusion(f32[4096,384]{1,0:T(8,128)S(1)} %fusion.11, f32[4096,384]{1,0:T(8,128)S(1)} %copy-done.7, bf16[1,4096,768]{2,1,0:T(8,128)(2,1)S(1)} %copy-done.6, s32[]{:T(128)S(6)} %select_n.13, bf16[8,768]{1,0:T(8,128)(2,1)S(1)} %collective-permute-done.1, bf16[4096,768]{1,0:T(8,128)(2,1)S(1)} %bitcast.72, ...), kind=kOutput, calls=%fused_computation.9 | convolution fusion | flops 2448949248 | bytes 25767940 | tf_op jit(solution)/shard_map/dot_general | solution.py:36
  38.2 0.0 all-gather.4.cloned.1.call-update
  38.2 0.0 all-gather.6.cloned.1.call-start
  38.2 0.7 all-gather.6.cloned.1.call-update
  38.9 0.0 reduce-scatter.2.cloned.1.call-start
  39.0 0.0 copy-done.4
  39.0 0.0 copy-done.5
  39.0 0.1 fusion.44
  39.1 18.2 %all-gather.4.cloned.1.call-done = bf16[4096,768]{1,0:T(8,128)(2,1)} async-done(((bf16[4096,384]{1,0:T(8,128)(2,1)}), bf16[4096,768]{1,0:T(8,128)(2,1)}) %all-gather.4.cloned.1.call-update) | async-done | bytes 6291472 | tf_op jit(solution)/shard_map/all_gather | solution.py:70
  57.3 10.0 %dot_general.40 = bf16[32,64,1536]{2,1,0:T(8,128)(2,1)} reshape(bf16[4096,768]{1,0:T(8,128)(2,1)} %all-gather.4.cloned.1.call-done) | data formatting | bytes 12582912 | tf_op jit(solution)/shard_map/dot_general | solution.py:74
  67.3 0.0 copy-done
  67.3 0.0 copy-start.1
  67.3 0.0 copy-start.2
  67.3 8.5 %convolution_reduce_fusion = bf16[32,768]{1,0:T(8,128)(2,1)S(1)} fusion(bf16[32,64,1536]{2,1,0:T(8,128)(2,1)} %dot_general.40, bf16[1536,768,1]{1,0,2:T(8,128)(2,1)S(1)} %bitcast.66), kind=kOutput, calls=%fused_computation.16 | convolution fusion | flops 4833386496 | bytes 8699904 | tf_op jit(solution)/shard_map/dot_general | solution.py:74
  75.8 0.0 copy-start.3
  75.8 2.0 %all_gather.19 = bf16[32,1536]{1,0:T(8,128)(2,1)S(1)} all-gather(bf16[32,768]{1,0:T(8,128)(2,1)S(1)} %convolution_reduce_fusion), channel_id=1, replica_groups=mesh['seq'=4,'section'=2,'batch'=4] {'section'}, dimensions={1}, use_global_device_ids=true | all-gather | bytes 147456 | tf_op jit(solution)/shard_map/all_gather | solution.py:80
  77.8 0.1 convert_reduce_fusion
  77.9 0.2 fusion.31
  78.2 0.0 copy-done.1
  78.2 0.0 copy-done.2
  78.2 0.6 convolution_convert_fusion
  78.7 14.6 %all_gather.21 = bf16[128,768]{1,0:T(8,128)(2,1)S(1)} all-gather(bf16[32,768]{1,0:T(8,128)(2,1)S(1)} %convolution_convert_fusion), channel_id=1, replica_groups=mesh['seq'=4,'section'=2,'batch'=4] {'seq'}, dimensions={0}, use_global_device_ids=true | all-gather | bytes 245760 | tf_op jit(solution)/shard_map/all_gather | solution.py:101
  93.3 0.2 copy.19
  93.5 1.8 %convolution_convert_fusion.1 = bf16[32,512]{1,0:T(8,128)(2,1)S(1)} fusion(bf16[1536,512]{1,0:T(8,128)(2,1)} %param.17, bf16[32,1536]{1,0:T(8,128)(2,1)S(1)} %all_gather.19, f32[1536]{0:T(1024)S(1)} %copy-done.2, f32[32]{0:T(128)S(1)} %add_rsqrt_fusion, f32[32]{0:T(128)S(1)} %broadcast_multiply_fusion), kind=kOutput, calls=%fused_computation.27 | convolution fusion | flops 50593792 | bytes 1710336 | tf_op jit(solution)/shard_map/dot_general | solution.py:89
  95.3 13.7 %all_gather.20 = bf16[128,512]{1,0:T(8,128)(2,1)S(1)} all-gather(bf16[32,512]{1,0:T(8,128)(2,1)S(1)} %convolution_convert_fusion.1), channel_id=1, replica_groups=mesh['seq'=4,'section'=2,'batch'=4] {'seq'}, dimensions={0}, use_global_device_ids=true | all-gather | bytes 163840 | tf_op jit(solution)/shard_map/all_gather | solution.py:100
  108.9 1.8 %fusion.19 = bf16[4,4,8,128]{3,2,1,0:T(8,128)(2,1)S(1)} fusion(bf16[1536,512]{1,0:T(8,128)(2,1)} %param.16, bf16[32,1536]{1,0:T(8,128)(2,1)S(1)} %all_gather.19, f32[1536]{0:T(1024)S(1)} %copy-done.2, f32[32]{0:T(128)S(1)} %add_rsqrt_fusion, f32[32]{0:T(128)S(1)} %broadcast_multiply_fusion), kind=kOutput, calls=%fused_computation.28 | convolution fusion | flops 50610176 | bytes 1710336 | tf_op jit(solution)/shard_map/dot_general | solution.py:87
  110.8 0.0 copy-done.3
  110.8 0.2 fusion.55
  111.0 0.2 fusion.35
  111.2 0.3 fusion.16
  111.5 0.1 copy.20
  111.6 0.1 convert_element_type.50
  111.7 2.9 %fusion.56 = f32[32,1536]{1,0:T(8,128)} fusion(bf16[32,768]{1,0:T(8,128)(2,1)S(1)} %convert_element_type.50, bf16[768,1536]{1,0:T(8,128)(2,1)} %param.19), kind=kOutput, calls=%fused_computation.70 | convolution fusion | flops 75497472 | bytes 2605056 | tf_op jit(solution)/shard_map/dot_general | solution.py:126
  114.5 48.8 %all_gather.22 = bf16[512,768]{1,0:T(8,128)(2,1)S(1)} all-gather(bf16[32,768]{1,0:T(8,128)(2,1)S(1)} %convert_element_type.50), channel_id=1, replica_groups=mesh['seq'=4,'section'=2,'batch'=4] {'batch','seq'}, dimensions={0}, use_global_device_ids=true | all-gather | bytes 835584 | tf_op jit(solution)/shard_map/all_gather | solution.py:130
  163.3 0.1 fusion.32
  163.4 0.0 reduce-scatter.2.cloned.1.call-update
  163.4 0.0 all-gather.6.cloned.1.call-done
  163.5 5.0 %fusion.13 = f32[768,1536]{1,0:T(8,128)} fusion(bf16[512,768]{1,0:T(8,128)(2,1)S(1)} %all_gather.22, bf16[1,512,1536]{2,1,0:T(8,128)(2,1)} %all-gather.6.cloned.1.call-done), kind=kOutput, calls=%fused_computation.17 | convolution fusion | flops 1207959552 | bytes 7077888 | tf_op jit(solution)/shard_map/dot_general | solution.py:131
  168.5 0.0 reduce-scatter.2.cloned.1.call-done
  168.5 1.5 fusion.37
  (3 shorter events, 0.0 us)
Async XLA Ops:
  7.2 60.1 %copy-start = (bf16[2,768,768]{2,1,0:T(8,128)(2,1)S(1)}, bf16[2,768,768]{2,1,0:T(8,128)(2,1)}, u32[]{:S(2)}) copy-start(bf16[2,768,768]{2,1,0:T(8,128)(2,1)} %param.14) | copy-start | bytes 7077892
  7.2 50.1 %all-gather.4.cloned.1.call-start = ((), (), s32[]{:S(2)}) async-start(), calls=%async_computation.1 | async-start | bytes 9437184 | tf_op jit(solution)/shard_map/all_gather | solution.py:70
  8.1 15.2 %collective-permute-start = (bf16[8,768]{1,0:T(8,128)(2,1)S(1)}, bf16[8,768]{1,0:T(8,128)(2,1)S(1)}, u32[]{:S(2)}, u32[]{:S(2)}) collective-permute-start(bf16[8,768]{1,0:T(8,128)(2,1)S(1)} %get-tuple-element.3), channel_id=1, source_target_pairs={{0,8},{8,16},{16,24},{1,9},{9,17},{17,25},{2,10},{10,18},{18,26},{... | collective-permute-start | bytes 36872 | tf_op jit(solution)/shard_map/ppermute | solution.py:19
  13.0 16.7 %collective-permute-start.1 = (bf16[8,768]{1,0:T(8,128)(2,1)S(1)}, bf16[8,768]{1,0:T(8,128)(2,1)S(1)}, u32[]{:S(2)}, u32[]{:S(2)}) collective-permute-start(bf16[8,768]{1,0:T(8,128)(2,1)S(1)} %get-tuple-element.2), channel_id=1, source_target_pairs={{8,0},{16,8},{24,16},{9,1},{17,9},{25,17},{10,2},{18,10},{26,18},{... | collective-permute-start | bytes 36872 | tf_op jit(solution)/shard_map/ppermute | solution.py:20
  23.3 6.5 %copy-start.6 = (bf16[1,4096,768]{2,1,0:T(8,128)(2,1)S(1)}, bf16[1,4096,768]{2,1,0:T(8,128)(2,1)}, u32[]{:S(2)}) copy-start(bf16[1,4096,768]{2,1,0:T(8,128)(2,1)} %param.12) | copy-start | bytes 18874372
  23.3 6.6 %copy-start.7 = (f32[4096,384]{1,0:T(8,128)S(1)}, f32[4096,384]{1,0:T(8,128)}, u32[]{:S(2)}) copy-start(f32[4096,384]{1,0:T(8,128)} %fusion.23) | copy-start | bytes 18874372
  29.7 9.3 %copy-start.4 = (s32[1,32]{1,0:T(1,128)S(1)}, s32[1,32]{1,0:T(1,128)}, u32[]{:S(2)}) copy-start(s32[1,32]{1,0:T(1,128)} %param.22) | copy-start | bytes 388
  29.7 9.3 %copy-start.5 = (s32[1,32]{1,0:T(1,128)S(1)}, s32[1,32]{1,0:T(1,128)}, u32[]{:S(2)}) copy-start(s32[1,32]{1,0:T(1,128)} %param.21) | copy-start | bytes 388
  38.2 125.3 %all-gather.6.cloned.1.call-start = ((), (), s32[]{:S(2)}) async-start(), calls=%async_computation.3 | async-start | bytes 1671168 | tf_op jit(solution)/shard_map/all_gather | solution.py:59
  38.9 129.5 %reduce-scatter.2.cloned.1.call-start = ((), (), s32[]{:S(2)}) async-start(), calls=%async_computation.2 | async-start | bytes 294912 | tf_op jit(solution)/shard_map/reduce_scatter | solution.py:127
  67.3 10.9 %copy-start.1 = (bf16[1536,768]{1,0:T(8,128)(2,1)S(1)}, bf16[1536,768]{1,0:T(8,128)(2,1)}, u32[]{:S(2)}) copy-start(bf16[1536,768]{1,0:T(8,128)(2,1)} %param.18) | copy-start | bytes 7077892
  67.3 10.9 %copy-start.2 = (f32[1536]{0:T(1024)S(1)}, f32[1536]{0:T(1024)}, u32[]{:S(2)}) copy-start(f32[1536]{0:T(1024)} %param.15) | copy-start | bytes 18436
  75.8 35.0 %copy-start.3 = (f32[1,4,32,128]{3,2,1,0:T(8,128)S(1)}, f32[1,4,32,128]{3,2,1,0:T(8,128)}, u32[]{:S(2)}) copy-start(f32[1,4,32,128]{3,2,1,0:T(8,128)} %param.20) | copy-start | bytes 196612
Sparse Core Ops, SparseCore 0:
  38.3 18.9 all-gather.3
  60.1 59.7 all-gather.5
  163.6 3.6 reduce-scatter.1

commit v2 on v0

v2 whole, which is shorter than its diff:
```python
import functools

import jax
import jax.numpy as jnp
from jax import lax
from jax.experimental import pallas as pl
from jax.experimental.pallas import tpu as pltpu
from jax.sharding import PartitionSpec as P

KEY = 128
VAL = 192
POOL = 128
STEP = 8
EDGE = 16
MESH = pl.DeviceIdType.MESH
LIMIT = 56 * 1024 * 1024


def conv_kernel(
    nseq, features, dil, strd, out, x, wd, ws, hs, hp, pooled, local_sem, send_sem, recv_sem
):
    s = lax.axis_index("seq")
    c = lax.axis_index("section")
    b = lax.axis_index("batch")
    length, width = features.shape
    half_rows = length // 2
    part = dil.shape[1]
    cols = strd.shape[1]
    peer = (s, 1 - c, b)
    after = (lax.rem(s + 1, nseq), c, b)
    before = (lax.rem(s + nseq - 1, nseq), c, b)
    halo_target = (lax.rem(s + 1 - 2 * c + nseq, nseq), c, b)

    load_x = pltpu.make_async_copy(
        features.at[pl.ds(pl.multiple_of(c * (half_rows - EDGE), EDGE), half_rows + EDGE)],
        x.at[pl.ds(pl.multiple_of(EDGE * (1 - c), EDGE), half_rows + EDGE)],
        local_sem.at[0],
    )
    load_d = pltpu.make_async_copy(dil, wd.at[0], local_sem.at[1])
    load_s = pltpu.make_async_copy(strd, ws.at[0], local_sem.at[2])
    load_d.start()
    load_x.start()

    barrier = pltpu.get_barrier_semaphore()
    for device in (peer, after, before):
        pl.semaphore_signal(barrier, inc=1, device_id=device, device_id_type=MESH)
    pl.semaphore_wait(barrier, 3)

    edge_row = pl.multiple_of(c * (half_rows + EDGE), EDGE)
    halo = pltpu.make_async_remote_copy(
        src_ref=features.at[pl.ds(pl.multiple_of((1 - c) * (length - EDGE), EDGE), EDGE)],
        dst_ref=x.at[pl.ds(edge_row, EDGE)],
        send_sem=send_sem.at[0],
        recv_sem=recv_sem.at[0],
        device_id=halo_target,
        device_id_type=MESH,
    )
    send_d = pltpu.make_async_remote_copy(
        src_ref=dil,
        dst_ref=wd.at[1],
        send_sem=send_sem.at[1],
        recv_sem=recv_sem.at[1],
        device_id=peer,
        device_id_type=MESH,
    )
    send_s = pltpu.make_async_remote_copy(
        src_ref=strd,
        dst_ref=ws.at[1],
        send_sem=send_sem.at[2],
        recv_sem=recv_sem.at[2],
        device_id=peer,
        device_id_type=MESH,
    )
    halo.start()
    send_d.start()
    send_s.start()
    load_s.start()

    load_x.wait()
    load_d.wait()
    halo.wait()
    outside = ((c == 0) & (s == 0)) | ((c == 1) & (s == nseq - 1))
    keep = jnp.where(outside, 0.0, 1.0).astype(jnp.float32)
    edge = x[pl.ds(edge_row, EDGE), :].astype(jnp.float32) * keep
    x[pl.ds(edge_row, EDGE), :] = edge.astype(jnp.bfloat16)

    chunk = hs.shape[2]
    lane_blocks = part // 128

    def dilated(slot, half):
        first = pl.multiple_of(half * part, 128)

        def body(i, carry):
            row = pl.multiple_of(i * chunk, chunk)
            block = x[pl.ds(row, chunk + 2 * EDGE), :]
            taps = jnp.concatenate(
                [block[EDGE + d : EDGE + d + chunk] for d in (-STEP, 0, STEP)], axis=1
            )
            preact = jnp.dot(taps, wd[slot], preferred_element_type=jnp.float32)
            own = x[pl.ds(row + EDGE, chunk), pl.ds(first, part)].astype(jnp.float32)
            hidden = own + jax.nn.gelu(preact)
            at = lax.rem(i, 2)
            for j in range(lane_blocks):
                hs[at, j] = hidden[:, 128 * j : 128 * (j + 1)]
            target = pl.multiple_of(i * (chunk // 2), chunk // 2)
            for parity in range(2):
                for j in range(lane_blocks):
                    lane = pl.multiple_of(first + parity * width + 128 * j, 128)
                    hp[pl.ds(target, chunk // 2), pl.ds(lane, 128)] = hs[
                        at, j, pl.ds(parity, chunk // 2, 2), :
                    ].astype(jnp.bfloat16)
            return carry

        lax.fori_loop(0, half_rows // chunk, body, 0, unroll=2)

    def strided(slot, half):
        rows = 8 * (POOL // 2)
        block_cols = 256
        per = cols // block_cols

        def body(k, carry):
            i, n = k // per, lax.rem(k, per)
            lane = pl.multiple_of(n * block_cols, block_cols)
            product = jnp.dot(
                hp[pl.ds(pl.multiple_of(i * rows, rows), rows), :],
                ws[slot, :, pl.ds(lane, block_cols)],
                preferred_element_type=jnp.float32,
            )
            best = product.reshape(8, POOL // 2, block_cols).max(axis=1)
            pooled[
                pl.ds(pl.multiple_of(i * 8, 8), 8),
                pl.ds(pl.multiple_of(half * cols + lane, 128), block_cols),
            ] = best
            return carry

        lax.fori_loop(0, half_rows // 2 // rows * per, body, 0)

    dilated(0, c)
    send_d.wait()
    dilated(1, 1 - c)
    load_s.wait()
    strided(0, c)
    send_s.wait()
    strided(1, 1 - c)
    out[...] = pooled[...].astype(jnp.bfloat16)


def conv(nseq, features, dil, strd):
    length, width = features.shape
    part = dil.shape[1]
    cols = strd.shape[1]
    rows = length // 2 // POOL
    chunk = 256
    hbm = pl.BlockSpec(memory_space=pl.ANY)
    return pl.pallas_call(
        functools.partial(conv_kernel, nseq),
        out_shape=jax.ShapeDtypeStruct((rows, 2 * cols), jnp.bfloat16),
        in_specs=[hbm, hbm, hbm],
        out_specs=pl.BlockSpec(memory_space=pltpu.VMEM),
        scratch_shapes=[
            pltpu.VMEM((length // 2 + 2 * EDGE, width), jnp.bfloat16),
            pltpu.VMEM((2,) + dil.shape, jnp.bfloat16),
            pltpu.VMEM((2,) + strd.shape, jnp.bfloat16),
            pltpu.VMEM((2, part // 128, chunk, 128), jnp.float32),
            pltpu.VMEM((length // 4, 2 * width), jnp.bfloat16),
            pltpu.VMEM((rows, 2 * cols), jnp.float32),
            pltpu.SemaphoreType.DMA((3,)),
            pltpu.SemaphoreType.DMA((3,)),
            pltpu.SemaphoreType.DMA((3,)),
        ],
        compiler_params=pltpu.CompilerParams(
            collective_id=0, has_side_effects=True, vmem_limit_bytes=LIMIT
        ),
        cost_estimate=pl.CostEstimate(
            flops=12_000_000_000, bytes_accessed=8_000_000, transcendentals=1_600_000
        ),
    )(features, dil, strd)


def attention_kernel(
    nseq,
    nbatch,
    pooled,
    gain,
    query_w,
    key_w,
    value_w,
    output_w,
    bias,
    lower,
    upper,
    layer_out,
    att,
    pool2,
    wq,
    wk,
    wv,
    wo,
    kv,
    proj,
    other,
    local_sem,
    pair_send,
    pair_recv,
    kv_send,
    kv_recv,
    att_send,
    att_recv,
):
    s = lax.axis_index("seq")
    c = lax.axis_index("section")
    b = lax.axis_index("batch")
    total = nseq * nbatch
    me = b * nseq + s
    half_rows = pooled.shape[0]
    rows = 2 * half_rows
    key_cols = key_w.shape[1]
    val_cols = value_w.shape[1]
    heads = key_cols // KEY
    out_cols = layer_out.shape[1]
    peer = (s, 1 - c, b)

    loads = [
        pltpu.make_async_copy(src, dst, local_sem.at[k])
        for k, (src, dst) in enumerate(
            ((key_w, wk), (value_w, wv), (query_w, wq), (output_w, wo))
        )
    ]
    for load in loads:
        load.start()

    barrier = pltpu.get_barrier_semaphore()
    pl.semaphore_signal(barrier, inc=1, device_id=peer, device_id_type=MESH)

    def greet(k, carry):
        t = lax.rem(me + k, total)
        pl.semaphore_signal(
            barrier, inc=1, device_id=(lax.rem(t, nseq), c, t // nseq), device_id_type=MESH
        )
        return carry

    lax.fori_loop(1, total, greet, 0)
    pl.semaphore_wait(barrier, total)

    mine = pl.ds(pl.multiple_of(c * half_rows, EDGE), half_rows)
    pool2[mine, :] = pooled[...]
    swap = pltpu.make_async_remote_copy(
        src_ref=pooled,
        dst_ref=pool2.at[mine],
        send_sem=pair_send.at[0],
        recv_sem=pair_recv.at[0],
        device_id=peer,
        device_id_type=MESH,
    )
    swap.start()
    swap.wait()

    values = pool2[...].astype(jnp.float32)
    centred = values - jnp.mean(values, axis=1, keepdims=True)
    spread = jnp.mean(centred * centred, axis=1, keepdims=True)
    normed = centred * lax.rsqrt(spread + 1e-05) * gain[...]
    proj[...] = normed
    inputs = normed.astype(jnp.bfloat16)
    here = pl.ds(pl.multiple_of(s * rows, rows), rows)
    loads[0].wait()
    kv[here, 0:key_cols] = jnp.dot(
        inputs, wk[...], preferred_element_type=jnp.float32
    ).astype(jnp.bfloat16)
    loads[1].wait()
    kv[here, key_cols : key_cols + val_cols] = jnp.dot(
        inputs, wv[...], preferred_element_type=jnp.float32
    ).astype(jnp.bfloat16)

    def kv_copy(k, owner):
        return pltpu.make_async_remote_copy(
            src_ref=kv.at[here],
            dst_ref=kv.at[pl.ds(pl.multiple_of(owner * rows, rows), rows)],
            send_sem=kv_send.at[k],
            recv_sem=kv_recv.at[k],
            device_id=(lax.rem(s + k, nseq), c, b),
            device_id_type=MESH,
        )

    def kv_start(k, carry):
        kv_copy(k, s).start()
        return carry

    def kv_wait(k, carry):
        kv_copy(k, s).wait_send()
        kv_copy(k, lax.rem(s + nseq - k, nseq)).wait_recv()
        return carry

    lax.fori_loop(1, nseq, kv_start, 0)
    loads[2].wait()
    query = (
        jnp.dot(inputs, wq[...], preferred_element_type=jnp.float32) * KEY ** (-0.5)
    ).astype(jnp.bfloat16)
    lax.fori_loop(1, nseq, kv_wait, 0)

    count = kv.shape[0]
    positions = lax.broadcasted_iota(jnp.int32, (rows, count), 1)
    visible = (positions >= lower[...]) & (positions < upper[...])
    lane = lax.broadcasted_iota(jnp.int32, (rows, 128), 1)
    pieces = []
    for pair in range(heads // 2):
        results = []
        for side in range(2):
            h = 2 * pair + side
            scores = lax.dot_general(
                query[:, h * KEY : (h + 1) * KEY],
                kv[:, h * KEY : (h + 1) * KEY],
                (((1,), (1,)), ((), ())),
                preferred_element_type=jnp.float32,
            )
            scores = jnp.where(visible, scores + bias[h], jnp.float32(-1e30))
            newest = jnp.max(scores, axis=1, keepdims=True)
            weights = jnp.where(visible, jnp.exp(scores - newest), jnp.float32(0.0))
            weight_sum = jnp.sum(weights, axis=1, keepdims=True)
            first = key_cols + pair * 2 * VAL + side * 128
            accum = jnp.dot(
                weights.astype(jnp.bfloat16),
                kv[:, first : first + 256],
                preferred_element_type=jnp.float32,
            )
            results.append(accum / weight_sum)
        left, right = results
        pieces += [
            left[:, :128],
            jnp.where(lane < VAL - 128, left[:, 128:], right[:, :128]),
            right[:, 128:],
        ]
    attended = jnp.concatenate(pieces, axis=1).astype(jnp.bfloat16)
    own_rows = pl.ds(pl.multiple_of(me * rows, rows), rows)
    att[own_rows, :] = attended

    def att_copy(k, owner):
        t = lax.rem(me + k, total)
        return pltpu.make_async_remote_copy(
            src_ref=att.at[own_rows],
            dst_ref=att.at[pl.ds(pl.multiple_of(owner * rows, rows), rows)],
            send_sem=att_send.at[k],
            recv_sem=att_recv.at[k],
            device_id=(lax.rem(t, nseq), c, t // nseq),
            device_id_type=MESH,
        )

    def att_start(k, carry):
        att_copy(k, me).start()
        return carry

    def att_wait(k, carry):
        att_copy(k, me).wait_send()
        att_copy(k, lax.rem(me + total - k, total)).wait_recv()
        return carry

    lax.fori_loop(1, total, att_start, 0)
    loads[3].wait()
    own_cols = pl.ds(pl.multiple_of(c * out_cols, 128), out_cols)
    peer_cols = pl.ds(pl.multiple_of((1 - c) * out_cols, 128), out_cols)
    other[0] = jnp.dot(attended, wo[:, peer_cols], preferred_element_type=jnp.float32)
    swap_out = pltpu.make_async_remote_copy(
        src_ref=other.at[0],
        dst_ref=other.at[1],
        send_sem=pair_send.at[1],
        recv_sem=pair_recv.at[1],
        device_id=peer,
        device_id_type=MESH,
    )
    swap_out.start()
    own = jnp.dot(attended, wo[:, own_cols], preferred_element_type=jnp.float32)
    swap_out.wait()
    layer_out[...] = (proj[:, own_cols] + (own + other[1])).astype(jnp.bfloat16)
    lax.fori_loop(1, total, att_wait, 0)


def attention(nseq, nbatch, pooled, gain, wq, wk, wv, wo, bias, lower, upper):
    rows = 2 * pooled.shape[0]
    channels = pooled.shape[1]
    total = nseq * nbatch
    cols = channels // 2
    hbm = pl.BlockSpec(memory_space=pl.ANY)
    vmem = pl.BlockSpec(memory_space=pltpu.VMEM)
    return pl.pallas_call(
        functools.partial(attention_kernel, nseq, nbatch),
        out_shape=(
            jax.ShapeDtypeStruct((rows, cols), jnp.bfloat16),
            jax.ShapeDtypeStruct((total * rows, wv.shape[1]), jnp.bfloat16),
        ),
        in_specs=[vmem, vmem, hbm, hbm, hbm, hbm, vmem, vmem, vmem],
        out_specs=(vmem, vmem),
        scratch_shapes=[
            pltpu.VMEM((rows, channels), jnp.bfloat16),
            pltpu.VMEM(wq.shape, jnp.bfloat16),
            pltpu.VMEM(wk.shape, jnp.bfloat16),
            pltpu.VMEM(wv.shape, jnp.bfloat16),
            pltpu.VMEM(wo.shape, jnp.bfloat16),
            pltpu.VMEM((nseq * rows, wk.shape[1] + wv.shape[1]), jnp.bfloat16),
            pltpu.VMEM((rows, channels), jnp.float32),
            pltpu.VMEM((2, rows, cols), jnp.float32),
            pltpu.SemaphoreType.DMA((4,)),
            pltpu.SemaphoreType.DMA((2,)),
            pltpu.SemaphoreType.DMA((2,)),
            pltpu.SemaphoreType.DMA((nseq,)),
            pltpu.SemaphoreType.DMA((nseq,)),
            pltpu.SemaphoreType.DMA((total,)),
            pltpu.SemaphoreType.DMA((total,)),
        ],
        compiler_params=pltpu.CompilerParams(
            collective_id=1, has_side_effects=True, vmem_limit_bytes=LIMIT
        ),
        cost_estimate=pl.CostEstimate(
            flops=400_000_000, bytes_accessed=9_000_000, transcendentals=20_000
        ),
    )(pooled, gain, wq, wk, wv, wo, bias, lower, upper)


def solution(mesh):
    nseq, nbatch = mesh.shape["seq"], mesh.shape["batch"]

    def shards(
        features,
        dilated_tap_weight,
        strided_weight,
        norm_gain,
        query_weight,
        key_weight,
        value_weight,
        output_weight,
        position_bias,
        interval_start,
        interval_end,
        cotangent,
    ):
        cotangent_all = lax.all_gather(cotangent[0], ("batch", "seq"), axis=0, tiled=True)
        width = features.shape[2]
        pooled = conv(
            nseq,
            features[0],
            dilated_tap_weight.reshape(3 * width, -1),
            strided_weight.reshape(2 * width, -1),
        )
        layer_out, attended = attention(
            nseq,
            nbatch,
            pooled,
            norm_gain[None],
            query_weight,
            key_weight,
            value_weight,
            output_weight,
            position_bias[0],
            interval_start[0][:, None],
            interval_end[0][:, None],
        )
        output_grad = lax.dot_general(
            attended,
            cotangent_all,
            (((0,), (0,)), ((), ())),
            preferred_element_type=jnp.float32,
        )
        return (layer_out[None], output_grad)

    return jax.shard_map(
        shards,
        mesh=mesh,
        in_specs=(
            P("batch", "seq", None),
            P(None, None, "section"),
            P(None, None, "section"),
            P(),
            P(None, "section"),
            P(None, "section"),
            P(None, "section"),
            P("section", None),
            P("batch", "section", "seq", None),
            P("batch", "seq"),
            P("batch", "seq"),
            P("batch", "seq", None),
        ),
        out_specs=(P("batch", "seq", "section"), P("section", None)),
        check_vma=False,
    )
```

time: 319 us -> 97.6 us (0.31)
  waiting for transfers between devices: 210 us -> 0.7 us
  Pallas kernels: 0 us -> 72.7 us
  matrix products: 39.7 us -> 5.26 us
  blocking collectives: 29.7 us -> 0 us
  local copies, waits for them, and re-layouts: 16.3 us -> 4.59 us
  starting transfers between devices: 6.33 us -> 0.04 us
    psum x1 -> x0, waiting for transfers between devices: 186 us -> none  [shards(): output_grad = lax.psum(grad_term, ('seq', 'batch'))]
    pallas_call x0 -> x2, Pallas kernels: none -> 72.7 us  [the longest x1 44.1 us: attention(): pl.pallas_call(functools.partial(attention_kernel, nseq, nbatch), out_sha...]
    dot_general x11 -> x1, matrix products: 39.7 us -> 5.26 us  [shards(): lax.dot_general(attended, cotangent_all, (((0,), (0,)), ((), ())), prefer...]
    all_gather x3 -> x0, blocking collectives: 29.7 us -> none  [the longest x1 13.9 us: shards(): value_piece = lax.all_gather(valued, 'seq', axis=0, tiled=True)]
    all_gather x1, waiting for transfers between devices: 18.9 us -> 0.02 us  [shards(): lax.all_gather(cotangent[0], ('batch', 'seq'), axis=0, tiled=True)]
    dot_general x1 -> x0, local copies, waits for them, and re-layouts: 10 us -> none  [shards(): strided = jnp.dot(paired, taps, preferred_element_type=jnp.float32)]
    ppermute x2 -> x0, starting transfers between devices: 6.21 us -> none  [the longest x1 4.92 us: padded(): before = lax.ppermute(last, axis, up)]
    reduce_scatter x1 -> x0, waiting for transfers between devices: 5.29 us -> none  [shards(): lax.psum_scatter(projected, 'section', scatter_dimension=1, tiled=True)]
  transfers between devices with their start and end apart: 5 -> 1, of which waited for: 3 -> 0; matrix products, arithmetic and copies ran while one was open for 6% -> 4% of each run, Pallas kernels for 0% -> 75%
where the time goes in v2:
time: 97.6 us; the launch traced here: 97.3 us
  Pallas kernels  72.7 us (74%)
  between operations  14.1 us (14%)
  matrix products  5.26 us (5%)
  local copies, waits for them, and re-layouts  4.59 us (5%)
    pallas_call x1, Pallas kernels, attention(): pl.pallas_call(functools.partial(attention_kernel, nseq, nbatch), out_sha...  44.1 us
    pallas_call x1, Pallas kernels, conv(): pl.pallas_call(functools.partial(conv_kernel, nseq), out_shape=jax.ShapeD...  28.6 us
    dot_general x1, matrix products, shards(): lax.dot_general(attended, cotangent_all, (((0,), (0,)), ((), ())), prefer...  5.26 us
  transfers between devices with their start and end apart: 1, of which 0 were waited for; matrix products, arithmetic and copies ran while one was open for 4% of the time, Pallas kernels for 75%

profile of v2, /device:TPU:0, one launch (start us, length us, event | category | flops | bytes accessed | tf_op | source)
XLA Modules:
  0.0 97.3 jit_solution(4453967501158667018)
XLA Ops:
  7.2 0.0 all-gather.3.cloned.1.call-start
  7.2 0.7 all-gather.3.cloned.1.call-update
  7.9 1.3 %broadcast_in_dim.6.gain = f32[1,1536]{1,0:T(1,128)} reshape(f32[1536]{0:T(1024)} %param.15) | data formatting | bytes 12288 | tf_op jit(solution)/shard_map/broadcast_in_dim | solution.py:446
  9.2 1.3 %copy.14.lower = s32[32,1]{1,0:T(8,128)} copy(s32[32,1]{0,1:T(1,128)} %bitcast.13) | data formatting | bytes 256 | tf_op jit(solution)/shard_map/broadcast_in_dim;squeeze | solution.py:452
  10.5 1.3 %copy.15.upper = s32[32,1]{1,0:T(8,128)} copy(s32[32,1]{0,1:T(1,128)} %bitcast.14) | data formatting | bytes 256 | tf_op jit(solution)/shard_map/broadcast_in_dim;squeeze | solution.py:453
  11.9 28.6 %shard_map.131.pooled = bf16[16,1536]{1,0:T(8,128)(2,1)} custom-call(bf16[4096,768]{1,0:T(8,128)(2,1)} %bitcast.15, bf16[2304,384]{1,0:T(8,128)(2,1)} %bitcast.17, bf16[1536,768]{1,0:T(8,128)(2,1)} %bitcast.16), custom_call_target="tpu_custom_call" | custom-call | flops 12000000000 | bytes 8000000 | tf_op jit(solution)/shard_map/pallas_call | solution.py:155
  40.5 44.1 %shard_map.132 = (bf16[32,768]{1,0:T(8,128)(2,1)}, bf16[512,768]{1,0:T(8,128)(2,1)}) custom-call(bf16[16,1536]{1,0:T(8,128)(2,1)} %shard_map.131.pooled, f32[1,1536]{1,0:T(1,128)} %broadcast_in_dim.6.gain, bf16[1536,512]{1,0:T(8,128)(2,1)} %query_w.1, bf16[1536,512]{1,0:T(8,128)(2,1)} %key_w.1, bf16[1536,768]{1,0:T(8,128)(2,1)} %value_w.1, ...), custom_call_target="tpu_custom_call" | custom-call | flops 400000000 | bytes 9000000 | tf_op jit(solution)/shard_map/pallas_call | solution.py:383
  84.6 0.0 all-gather.3.cloned.1.call-done
  84.6 0.0 copy-start
  84.6 5.3 %fusion = f32[768,1536]{1,0:T(8,128)} fusion(bf16[512,768]{1,0:T(8,128)(2,1)} %get-tuple-element.5, bf16[1,512,1536]{2,1,0:T(8,128)(2,1)} %all-gather.3.cloned.1.call-done), kind=kOutput, calls=%fused_computation | convolution fusion | flops 1207959552 | bytes 7077888 | tf_op jit(solution)/shard_map/dot_general | solution.py:455
  89.9 0.0 copy-done
  89.9 0.6 copy.17
Async XLA Ops:
  7.2 77.4 %all-gather.3.cloned.1.call-start = ((), (), s32[]{:S(2)}) async-start(), calls=%async_computation | async-start | bytes 1671168 | tf_op jit(solution)/shard_map/all_gather | solution.py:434
  84.6 5.3 %copy-start = (bf16[32,768]{1,0:T(8,128)(2,1)S(1)}, bf16[32,768]{1,0:T(8,128)(2,1)}, u32[]{:S(2)}) copy-start(bf16[32,768]{1,0:T(8,128)(2,1)} %get-tuple-element.4) | copy-start | bytes 147460
Sparse Core Ops, SparseCore 0:
  10.8 72.1 all-gather.2

commit v3 on v2

--- a/solution.py
+++ b/solution.py
@@ -16,8 +16,122 @@
 LIMIT = 56 * 1024 * 1024
 
 
+class Gather:
+    def __init__(self, nseq, nbatch, own, dst, rows, sems):
+        self.nseq, self.nbatch, self.own, self.dst, self.rows = nseq, nbatch, own, dst, rows
+        self.seq_send, self.seq_recv, self.batch_send, self.batch_recv = sems
+        self.s = lax.axis_index("seq")
+        self.c = lax.axis_index("section")
+        self.b = lax.axis_index("batch")
+
+    def slot(self, batch, seq):
+        row = pl.multiple_of((batch * self.nseq + seq) * self.rows, self.rows)
+        return self.dst.at[pl.ds(row, self.rows)]
+
+    def source(self, k):
+        return lax.rem(self.s + self.nseq - k, self.nseq)
+
+    def seq_copy(self, k, owner):
+        return pltpu.make_async_remote_copy(
+            src_ref=self.own,
+            dst_ref=self.slot(self.b, owner),
+            send_sem=self.seq_send.at[k],
+            recv_sem=self.seq_recv.at[k],
+            device_id=(lax.rem(self.s + k, self.nseq), self.c, self.b),
+            device_id_type=MESH,
+        )
+
+    def batch_copy(self, k, j, owner, src):
+        return pltpu.make_async_remote_copy(
+            src_ref=src,
+            dst_ref=self.slot(owner, self.source(k)),
+            send_sem=self.batch_send.at[k * self.nbatch + j],
+            recv_sem=self.batch_recv.at[k * self.nbatch + j],
+            device_id=(self.s, self.c, lax.rem(self.b + j, self.nbatch)),
+            device_id_type=MESH,
+        )
+
+    def start(self):
+        def seq(k, carry):
+            self.seq_copy(k, self.s).start()
+            return carry
+
+        def batch(j, carry):
+            self.batch_copy(0, j, self.b, self.own).start()
+            return carry
+
+        lax.fori_loop(1, self.nseq, seq, 0)
+        lax.fori_loop(1, self.nbatch, batch, 0)
+
+    def forward(self):
+        def seq(k, carry):
+            self.seq_copy(k, self.s).wait_send()
+            self.seq_copy(k, self.source(k)).wait_recv()
+
+            def batch(j, inner):
+                self.batch_copy(k, j, self.b, self.slot(self.b, self.source(k))).start()
+                return inner
+
+            return lax.fori_loop(1, self.nbatch, batch, carry)
+
+        lax.fori_loop(1, self.nseq, seq, 0)
+
+    def finish(self):
+        def seq(k, carry):
+            def batch(j, inner):
+                owner = lax.rem(self.b + self.nbatch - j, self.nbatch)
+                self.batch_copy(k, j, self.b, self.own).wait_send()
+                self.batch_copy(k, j, owner, self.own).wait_recv()
+                return inner
+
+            return lax.fori_loop(1, self.nbatch, batch, carry)
+
+        lax.fori_loop(0, self.nseq, seq, 0)
+
+
+def gather_semaphores(nseq, nbatch):
+    return [pltpu.SemaphoreType.DMA((n,)) for n in (nseq, nseq, nseq * nbatch, nseq * nbatch)]
+
+
+def enter(nseq, nbatch):
+    s, c, b = (lax.axis_index(name) for name in ("seq", "section", "batch"))
+    barrier = pltpu.get_barrier_semaphore()
+    pl.semaphore_signal(barrier, inc=1, device_id=(s, 1 - c, b), device_id_type=MESH)
+
+    def seq(k, carry):
+        device = (lax.rem(s + k, nseq), c, b)
+        pl.semaphore_signal(barrier, inc=1, device_id=device, device_id_type=MESH)
+        return carry
+
+    def batch(k, carry):
+        device = (s, c, lax.rem(b + k, nbatch))
+        pl.semaphore_signal(barrier, inc=1, device_id=device, device_id_type=MESH)
+        return carry
+
+    lax.fori_loop(1, nseq, seq, 0)
+    lax.fori_loop(1, nbatch, batch, 0)
+    pl.semaphore_wait(barrier, nseq + nbatch - 1)
+
+
 def conv_kernel(
-    nseq, features, dil, strd, out, x, wd, ws, hs, hp, pooled, local_sem, send_sem, recv_sem
+    nseq,
+    nbatch,
+    features,
+    dil,
+    strd,
+    cot,
+    out,
+    cot_half,
+    x,
+    wd,
+    ws,
+    hs,
+    hp,
+    pooled,
+    local_sem,
+    send_sem,
+    recv_sem,
+    *gather_sems,
 ):
     s = lax.axis_index("seq")
     c = lax.axis_index("section")
@@ -27,8 +141,6 @@
     part = dil.shape[1]
     cols = strd.shape[1]
     peer = (s, 1 - c, b)
-    after = (lax.rem(s + 1, nseq), c, b)
-    before = (lax.rem(s + nseq - 1, nseq), c, b)
     halo_target = (lax.rem(s + 1 - 2 * c + nseq, nseq), c, b)
 
     load_x = pltpu.make_async_copy(
@@ -41,10 +153,7 @@
     load_d.start()
     load_x.start()
 
-    barrier = pltpu.get_barrier_semaphore()
-    for device in (peer, after, before):
-        pl.semaphore_signal(barrier, inc=1, device_id=device, device_id_type=MESH)
-    pl.semaphore_wait(barrier, 3)
+    enter(nseq, nbatch)
 
     edge_row = pl.multiple_of(c * (half_rows + EDGE), EDGE)
     halo = pltpu.make_async_remote_copy(
@@ -75,6 +184,12 @@
     send_d.start()
     send_s.start()
     load_s.start()
+    cot_rows, cot_cols = cot.shape[0], cot_half.shape[1]
+    cot_own = cot.at[:, pl.ds(pl.multiple_of(c * cot_cols, 128), cot_cols)]
+    gather = Gather(nseq, nbatch, cot_own, cot_half, cot_rows, gather_sems)
+    keep_cot = pltpu.make_async_copy(cot_own, gather.slot(b, s), local_sem.at[3])
+    keep_cot.start()
+    gather.start()
 
     load_x.wait()
     load_d.wait()
@@ -137,15 +252,18 @@
 
     dilated(0, c)
     send_d.wait()
+    gather.forward()
     dilated(1, 1 - c)
     load_s.wait()
     strided(0, c)
     send_s.wait()
     strided(1, 1 - c)
     out[...] = pooled[...].astype(jnp.bfloat16)
-
-
-def conv(nseq, features, dil, strd):
+    keep_cot.wait()
+    gather.finish()
+
+
+def conv(nseq, nbatch, features, dil, strd, cot):
     length, width = features.shape
     part = dil.shape[1]
     cols = strd.shape[1]
@@ -153,10 +271,13 @@
     chunk = 256
     hbm = pl.BlockSpec(memory_space=pl.ANY)
     return pl.pallas_call(
-        functools.partial(conv_kernel, nseq),
-        out_shape=jax.ShapeDtypeStruct((rows, 2 * cols), jnp.bfloat16),
-        in_specs=[hbm, hbm, hbm],
-        out_specs=pl.BlockSpec(memory_space=pltpu.VMEM),
+        functools.partial(conv_kernel, nseq, nbatch),
+        out_shape=(
+            jax.ShapeDtypeStruct((rows, 2 * cols), jnp.bfloat16),
+            jax.ShapeDtypeStruct((nseq * nbatch * cot.shape[0], cot.shape[1] // 2), jnp.bfloat16),
+        ),
+        in_specs=[hbm, hbm, hbm, hbm],
+        out_specs=(pl.BlockSpec(memory_space=pltpu.VMEM), hbm),
         scratch_shapes=[
             pltpu.VMEM((length // 2 + 2 * EDGE, width), jnp.bfloat16),
             pltpu.VMEM((2,) + dil.shape, jnp.bfloat16),
@@ -164,17 +285,18 @@
             pltpu.VMEM((2, part // 128, chunk, 128), jnp.float32),
             pltpu.VMEM((length // 4, 2 * width), jnp.bfloat16),
             pltpu.VMEM((rows, 2 * cols), jnp.float32),
+            pltpu.SemaphoreType.DMA((4,)),
             pltpu.SemaphoreType.DMA((3,)),
             pltpu.SemaphoreType.DMA((3,)),
-            pltpu.SemaphoreType.DMA((3,)),
-        ],
+        ]
+        + gather_semaphores(nseq, nbatch),
         compiler_params=pltpu.CompilerParams(
             collective_id=0, has_side_effects=True, vmem_limit_bytes=LIMIT
         ),
         cost_estimate=pl.CostEstimate(
             flops=12_000_000_000, bytes_accessed=8_000_000, transcendentals=1_600_000
         ),
-    )(features, dil, strd)
+    )(features, dil, strd, cot)
 
 
 def attention_kernel(
@@ -189,8 +311,10 @@
     bias,
     lower,
     upper,
+    cot_half,
     layer_out,
     att,
+    cot_all,
     pool2,
     wq,
     wk,
@@ -204,13 +328,11 @@
     pair_recv,
     kv_send,
     kv_recv,
-    att_send,
-    att_recv,
+    *gather_sems,
 ):
     s = lax.axis_index("seq")
     c = lax.axis_index("section")
     b = lax.axis_index("batch")
-    total = nseq * nbatch
     me = b * nseq + s
     half_rows = pooled.shape[0]
     rows = 2 * half_rows
@@ -229,18 +351,7 @@
     for load in loads:
         load.start()
 
-    barrier = pltpu.get_barrier_semaphore()
-    pl.semaphore_signal(barrier, inc=1, device_id=peer, device_id_type=MESH)
-
-    def greet(k, carry):
-        t = lax.rem(me + k, total)
-        pl.semaphore_signal(
-            barrier, inc=1, device_id=(lax.rem(t, nseq), c, t // nseq), device_id_type=MESH
-        )
-        return carry
-
-    lax.fori_loop(1, total, greet, 0)
-    pl.semaphore_wait(barrier, total)
+    enter(nseq, nbatch)
 
     mine = pl.ds(pl.multiple_of(c * half_rows, EDGE), half_rows)
     pool2[mine, :] = pooled[...]
@@ -253,12 +364,25 @@
         device_id_type=MESH,
     )
     swap.start()
+    cot_cols = cot_half.shape[1]
+    cot_place = cot_all.at[:, pl.ds(pl.multiple_of(c * cot_cols, 128), cot_cols)]
+    keep_cot = pltpu.make_async_copy(cot_half, cot_place, local_sem.at[4])
+    swap_cot = pltpu.make_async_remote_copy(
+        src_ref=cot_half,
+        dst_ref=cot_place,
+        send_sem=pair_send.at[2],
+        recv_sem=pair_recv.at[2],
+        device_id=peer,
+        device_id_type=MESH,
+    )
     swap.wait()
+    keep_cot.start()
+    swap_cot.start()
 
     values = pool2[...].astype(jnp.float32)
     centred = values - jnp.mean(values, axis=1, keepdims=True)
     spread = jnp.mean(centred * centred, axis=1, keepdims=True)
-    normed = centred * lax.rsqrt(spread + 1e-05) * gain[...]
+    normed = centred * lax.rsqrt(spread + 1e-05) * gain[...].reshape(1, -1)
     proj[...] = normed
     inputs = normed.astype(jnp.bfloat16)
     here = pl.ds(pl.multiple_of(s * rows, rows), rows)
@@ -299,7 +423,12 @@
 
     count = kv.shape[0]
     positions = lax.broadcasted_iota(jnp.int32, (rows, count), 1)
-    visible = (positions >= lower[...]) & (positions < upper[...])
+    turn = lax.broadcasted_iota(jnp.int32, (rows, rows), 0) == lax.broadcasted_iota(
+        jnp.int32, (rows, rows), 1
+    )
+    low = jnp.sum(jnp.where(turn, lower[...], 0), axis=1, keepdims=True)
+    high = jnp.sum(jnp.where(turn, upper[...], 0), axis=1, keepdims=True)
+    visible = (positions >= low) & (positions < high)
     lane = lax.broadcasted_iota(jnp.int32, (rows, 128), 1)
     pieces = []
     for pair in range(heads // 2):
@@ -333,27 +462,8 @@
     own_rows = pl.ds(pl.multiple_of(me * rows, rows), rows)
     att[own_rows, :] = attended
 
-    def att_copy(k, owner):
-        t = lax.rem(me + k, total)
-        return pltpu.make_async_remote_copy(
-            src_ref=att.at[own_rows],
-            dst_ref=att.at[pl.ds(pl.multiple_of(owner * rows, rows), rows)],
-            send_sem=att_send.at[k],
-            recv_sem=att_recv.at[k],
-            device_id=(lax.rem(t, nseq), c, t // nseq),
-            device_id_type=MESH,
-        )
-
-    def att_start(k, carry):
-        att_copy(k, me).start()
-        return carry
-
-    def att_wait(k, carry):
-        att_copy(k, me).wait_send()
-        att_copy(k, lax.rem(me + total - k, total)).wait_recv()
-        return carry
-
-    lax.fori_loop(1, total, att_start, 0)
+    gather = Gather(nseq, nbatch, att.at[own_rows], att, rows, gather_sems)
+    gather.start()
     loads[3].wait()
     own_cols = pl.ds(pl.multiple_of(c * out_cols, 128), out_cols)
     peer_cols = pl.ds(pl.multiple_of((1 - c) * out_cols, 128), out_cols)
@@ -367,13 +477,16 @@
         device_id_type=MESH,
     )
     swap_out.start()
+    gather.forward()
     own = jnp.dot(attended, wo[:, own_cols], preferred_element_type=jnp.float32)
     swap_out.wait()
     layer_out[...] = (proj[:, own_cols] + (own + other[1])).astype(jnp.bfloat16)
-    lax.fori_loop(1, total, att_wait, 0)
-
-
-def attention(nseq, nbatch, pooled, gain, wq, wk, wv, wo, bias, lower, upper):
+    keep_cot.wait()
+    swap_cot.wait()
+    gather.finish()
+
+
+def attention(nseq, nbatch, pooled, gain, wq, wk, wv, wo, bias, lower, upper, cot_half):
     rows = 2 * pooled.shape[0]
     channels = pooled.shape[1]
     total = nseq * nbatch
@@ -385,9 +498,10 @@
         out_shape=(
             jax.ShapeDtypeStruct((rows, cols), jnp.bfloat16),
             jax.ShapeDtypeStruct((total * rows, wv.shape[1]), jnp.bfloat16),
-        ),
-        in_specs=[vmem, vmem, hbm, hbm, hbm, hbm, vmem, vmem, vmem],
-        out_specs=(vmem, vmem),
+            jax.ShapeDtypeStruct((total * rows, channels), jnp.bfloat16),
+        ),
+        in_specs=[vmem, vmem, hbm, hbm, hbm, hbm, vmem, vmem, vmem, hbm],
+        out_specs=(vmem, vmem, hbm),
         scratch_shapes=[
             pltpu.VMEM((rows, channels), jnp.bfloat16),
             pltpu.VMEM(wq.shape, jnp.bfloat16),
@@ -397,21 +511,20 @@
             pltpu.VMEM((nseq * rows, wk.shape[1] + wv.shape[1]), jnp.bfloat16),
             pltpu.VMEM((rows, channels), jnp.float32),
             pltpu.VMEM((2, rows, cols), jnp.float32),
-            pltpu.SemaphoreType.DMA((4,)),
-            pltpu.SemaphoreType.DMA((2,)),
-            pltpu.SemaphoreType.DMA((2,)),
+            pltpu.SemaphoreType.DMA((5,)),
+            pltpu.SemaphoreType.DMA((3,)),
+            pltpu.SemaphoreType.DMA((3,)),
             pltpu.SemaphoreType.DMA((nseq,)),
             pltpu.SemaphoreType.DMA((nseq,)),
-            pltpu.SemaphoreType.DMA((total,)),
-            pltpu.SemaphoreType.DMA((total,)),
-        ],
+        ]
+        + gather_semaphores(nseq, nbatch),
         compiler_params=pltpu.CompilerParams(
             collective_id=1, has_side_effects=True, vmem_limit_bytes=LIMIT
         ),
         cost_estimate=pl.CostEstimate(
             flops=400_000_000, bytes_accessed=9_000_000, transcendentals=20_000
         ),
-    )(pooled, gain, wq, wk, wv, wo, bias, lower, upper)
+    )(pooled, gain, wq, wk, wv, wo, bias, lower, upper, cot_half)
 
 
 def solution(mesh):
@@ -431,26 +544,28 @@
         interval_end,
         cotangent,
     ):
-        cotangent_all = lax.all_gather(cotangent[0], ("batch", "seq"), axis=0, tiled=True)
         width = features.shape[2]
-        pooled = conv(
+        pooled, cot_half = conv(
             nseq,
+            nbatch,
             features[0],
             dilated_tap_weight.reshape(3 * width, -1),
             strided_weight.reshape(2 * width, -1),
-        )
-        layer_out, attended = attention(
+            cotangent[0],
+        )
+        layer_out, attended, cotangent_all = attention(
             nseq,
             nbatch,
             pooled,
-            norm_gain[None],
+            norm_gain,
             query_weight,
             key_weight,
             value_weight,
             output_weight,
             position_bias[0],
-            interval_start[0][:, None],
-            interval_end[0][:, None],
+            interval_start,
+            interval_end,
+            cot_half,
         )
         output_grad = lax.dot_general(
             attended,

time: 97.6 us -> 67.3 us (0.69)
  between operations: 14.1 us -> 0.66 us
  Pallas kernels: 72.7 us -> 60.5 us
  local copies, waits for them, and re-layouts: 4.59 us -> 0.62 us
    pallas_call x1, Pallas kernels: 44.1 us -> 28.9 us  [attention(): pl.pallas_call(functools.partial(attention_kernel, nseq, nbatch), out_sha...]
    pallas_call x1, Pallas kernels: 28.6 us -> 31.7 us  [conv(): pl.pallas_call(functools.partial(conv_kernel, nseq, nbatch), out_shape=(j...]
    another operation x2 -> x0, local copies, waits for them, and re-layouts: 2.68 us -> none  [the longest x1 1.34 us: shards(): interval_start[0][:, None]]
    broadcast_in_dim x1 -> x0, local copies, waits for them, and re-layouts: 1.29 us -> none  [shards(): norm_gain[None]]
  transfers between devices with their start and end apart: 1 -> 0, of which waited for: 0 -> 0; matrix products, arithmetic and copies ran while one was open for 4% -> 0% of each run, Pallas kernels for 75% -> 0%
where the time goes in v3:
time: 67.3 us; the launch traced here: 67.1 us
  Pallas kernels  60.5 us (90%)
  matrix products  5.27 us (8%)
    pallas_call x1, Pallas kernels, conv(): pl.pallas_call(functools.partial(conv_kernel, nseq, nbatch), out_shape=(j...  31.7 us
    pallas_call x1, Pallas kernels, attention(): pl.pallas_call(functools.partial(attention_kernel, nseq, nbatch), out_sha...  28.9 us
    dot_general x1, matrix products, shards(): lax.dot_general(attended, cotangent_all, (((0,), (0,)), ((), ())), prefer...  5.27 us

profile of v3, /device:TPU:0, one launch (start us, length us, event | category | flops | bytes accessed | tf_op | source)
XLA Modules:
  0.0 67.1 jit_solution(14431119319913147530)
XLA Ops:
  0.6 31.7 %shard_map.131 = (bf16[16,1536]{1,0:T(8,128)(2,1)}, bf16[512,768]{1,0:T(8,128)(2,1)}) custom-call(bf16[4096,768]{1,0:T(8,128)(2,1)} %bitcast.10, bf16[2304,384]{1,0:T(8,128)(2,1)} %bitcast.12, bf16[1536,768]{1,0:T(8,128)(2,1)} %bitcast.11, bf16[32,1536]{1,0:T(8,128)(2,1)} %bitcast.13), custom_call_target="tpu_custom_call" | custom-call | flops 12000000000 | bytes 8000000 | tf_op jit(solution)/shard_map/pallas_call | solution.py:273
  32.3 28.9 %shard_map.132 = (bf16[32,768]{1,0:T(8,128)(2,1)}, bf16[512,768]{1,0:T(8,128)(2,1)}, bf16[512,1536]{1,0:T(8,128)(2,1)}) custom-call(bf16[16,1536]{1,0:T(8,128)(2,1)} %get-tuple-element.7.pooled, f32[1536]{0:T(1024)} %gain.1, bf16[1536,512]{1,0:T(8,128)(2,1)} %query_w.1, bf16[1536,512]{1,0:T(8,128)(2,1)} %key_w.1, bf16[1536,768]{1,0:T(8,128)(2,1)} %value_w.1, ...), custom_call_target="tpu_custom_call" | custom-call | flops 400000000 | bytes 9000000 | tf_op jit(solution)/shard_map/pallas_call | solution.py:496
  61.2 0.0 copy-start
  61.2 5.3 %fusion = f32[768,1536]{1,0:T(8,128)} fusion(bf16[512,768]{1,0:T(8,128)(2,1)} %get-tuple-element.10, bf16[512,1536]{1,0:T(8,128)(2,1)} %get-tuple-element.11), kind=kOutput, calls=%fused_computation | convolution fusion | flops 1207959552 | bytes 7077888 | tf_op jit(solution)/shard_map/dot_general | solution.py:570
  66.5 0.0 copy-done
  66.5 0.6 copy.15
Async XLA Ops:
  61.2 5.3 %copy-start = (bf16[32,768]{1,0:T(8,128)(2,1)S(1)}, bf16[32,768]{1,0:T(8,128)(2,1)}, u32[]{:S(2)}) copy-start(bf16[32,768]{1,0:T(8,128)(2,1)} %get-tuple-element.9) | copy-start | bytes 147460

commit v4 on v3

--- a/solution.py
+++ b/solution.py
@@ -17,7 +17,8 @@
 
 
 class Gather:
-    def __init__(self, nseq, nbatch, own, dst, rows, sems):
+    def __init__(self, nseq, nbatch, own, dst, rows, sems, lanes=slice(None)):
+        self.lanes = lanes
         self.nseq, self.nbatch, self.own, self.dst, self.rows = nseq, nbatch, own, dst, rows
         self.seq_send, self.seq_recv, self.batch_send, self.batch_recv = sems
         self.s = lax.axis_index("seq")
@@ -26,7 +27,7 @@
 
     def slot(self, batch, seq):
         row = pl.multiple_of((batch * self.nseq + seq) * self.rows, self.rows)
-        return self.dst.at[pl.ds(row, self.rows)]
+        return self.dst.at[pl.ds(row, self.rows), self.lanes]
 
     def source(self, k):
         return lax.rem(self.s + self.nseq - k, self.nseq)
@@ -121,7 +122,7 @@
     strd,
     cot,
     out,
-    cot_half,
+    cot_all,
     x,
     wd,
     ws,
@@ -184,9 +185,19 @@
     send_d.start()
     send_s.start()
     load_s.start()
-    cot_rows, cot_cols = cot.shape[0], cot_half.shape[1]
-    cot_own = cot.at[:, pl.ds(pl.multiple_of(c * cot_cols, 128), cot_cols)]
-    gather = Gather(nseq, nbatch, cot_own, cot_half, cot_rows, gather_sems)
+    cot_rows, cot_cols = cot.shape[0], cot.shape[1] // 2
+    cot_lanes = pl.ds(pl.multiple_of(c * cot_cols, 128), cot_cols)
+    cot_own = cot.at[:, cot_lanes]
+    cot_place = cot_all.at[:, cot_lanes]
+    gather = Gather(nseq, nbatch, cot_own, cot_all, cot_rows, gather_sems, cot_lanes)
+    swap_cot = pltpu.make_async_remote_copy(
+        src_ref=cot_place,
+        dst_ref=cot_place,
+        send_sem=send_sem.at[3],
+        recv_sem=recv_sem.at[3],
+        device_id=peer,
+        device_id_type=MESH,
+    )
     keep_cot = pltpu.make_async_copy(cot_own, gather.slot(b, s), local_sem.at[3])
     keep_cot.start()
     gather.start()
@@ -254,13 +265,15 @@
     send_d.wait()
     gather.forward()
     dilated(1, 1 - c)
+    keep_cot.wait()
+    gather.finish()
+    swap_cot.start()
     load_s.wait()
     strided(0, c)
     send_s.wait()
     strided(1, 1 - c)
     out[...] = pooled[...].astype(jnp.bfloat16)
-    keep_cot.wait()
-    gather.finish()
+    swap_cot.wait()
 
 
 def conv(nseq, nbatch, features, dil, strd, cot):
@@ -274,7 +287,7 @@
         functools.partial(conv_kernel, nseq, nbatch),
         out_shape=(
             jax.ShapeDtypeStruct((rows, 2 * cols), jnp.bfloat16),
-            jax.ShapeDtypeStruct((nseq * nbatch * cot.shape[0], cot.shape[1] // 2), jnp.bfloat16),
+            jax.ShapeDtypeStruct((nseq * nbatch * cot.shape[0], cot.shape[1]), jnp.bfloat16),
         ),
         in_specs=[hbm, hbm, hbm, hbm],
         out_specs=(pl.BlockSpec(memory_space=pltpu.VMEM), hbm),
@@ -286,8 +299,8 @@
             pltpu.VMEM((length // 4, 2 * width), jnp.bfloat16),
             pltpu.VMEM((rows, 2 * cols), jnp.float32),
             pltpu.SemaphoreType.DMA((4,)),
-            pltpu.SemaphoreType.DMA((3,)),
-            pltpu.SemaphoreType.DMA((3,)),
+            pltpu.SemaphoreType.DMA((4,)),
+            pltpu.SemaphoreType.DMA((4,)),
         ]
         + gather_semaphores(nseq, nbatch),
         compiler_params=pltpu.CompilerParams(
@@ -311,10 +324,8 @@
     bias,
     lower,
     upper,
-    cot_half,
     layer_out,
     att,
-    cot_all,
     pool2,
     wq,
     wk,
@@ -364,20 +375,7 @@
         device_id_type=MESH,
     )
     swap.start()
-    cot_cols = cot_half.shape[1]
-    cot_place = cot_all.at[:, pl.ds(pl.multiple_of(c * cot_cols, 128), cot_cols)]
-    keep_cot = pltpu.make_async_copy(cot_half, cot_place, local_sem.at[4])
-    swap_cot = pltpu.make_async_remote_copy(
-        src_ref=cot_half,
-        dst_ref=cot_place,
-        send_sem=pair_send.at[2],
-        recv_sem=pair_recv.at[2],
-        device_id=peer,
-        device_id_type=MESH,
-    )
     swap.wait()
-    keep_cot.start()
-    swap_cot.start()
 
     values = pool2[...].astype(jnp.float32)
     centred = values - jnp.mean(values, axis=1, keepdims=True)
@@ -481,12 +479,10 @@
     own = jnp.dot(attended, wo[:, own_cols], preferred_element_type=jnp.float32)
     swap_out.wait()
     layer_out[...] = (proj[:, own_cols] + (own + other[1])).astype(jnp.bfloat16)
-    keep_cot.wait()
-    swap_cot.wait()
     gather.finish()
 
 
-def attention(nseq, nbatch, pooled, gain, wq, wk, wv, wo, bias, lower, upper, cot_half):
+def attention(nseq, nbatch, pooled, gain, wq, wk, wv, wo, bias, lower, upper):
     rows = 2 * pooled.shape[0]
     channels = pooled.shape[1]
     total = nseq * nbatch
@@ -498,10 +494,9 @@
         out_shape=(
             jax.ShapeDtypeStruct((rows, cols), jnp.bfloat16),
             jax.ShapeDtypeStruct((total * rows, wv.shape[1]), jnp.bfloat16),
-            jax.ShapeDtypeStruct((total * rows, channels), jnp.bfloat16),
-        ),
-        in_specs=[vmem, vmem, hbm, hbm, hbm, hbm, vmem, vmem, vmem, hbm],
-        out_specs=(vmem, vmem, hbm),
+        ),
+        in_specs=[vmem, vmem, hbm, hbm, hbm, hbm, vmem, vmem, vmem],
+        out_specs=(vmem, vmem),
         scratch_shapes=[
             pltpu.VMEM((rows, channels), jnp.bfloat16),
             pltpu.VMEM(wq.shape, jnp.bfloat16),
@@ -511,9 +506,9 @@
             pltpu.VMEM((nseq * rows, wk.shape[1] + wv.shape[1]), jnp.bfloat16),
             pltpu.VMEM((rows, channels), jnp.float32),
             pltpu.VMEM((2, rows, cols), jnp.float32),
-            pltpu.SemaphoreType.DMA((5,)),
-            pltpu.SemaphoreType.DMA((3,)),
-            pltpu.SemaphoreType.DMA((3,)),
+            pltpu.SemaphoreType.DMA((4,)),
+            pltpu.SemaphoreType.DMA((2,)),
+            pltpu.SemaphoreType.DMA((2,)),
             pltpu.SemaphoreType.DMA((nseq,)),
             pltpu.SemaphoreType.DMA((nseq,)),
         ]
@@ -524,7 +519,7 @@
         cost_estimate=pl.CostEstimate(
             flops=400_000_000, bytes_accessed=9_000_000, transcendentals=20_000
         ),
-    )(pooled, gain, wq, wk, wv, wo, bias, lower, upper, cot_half)
+    )(pooled, gain, wq, wk, wv, wo, bias, lower, upper)
 
 
 def solution(mesh):
@@ -545,7 +540,7 @@
         cotangent,
     ):
         width = features.shape[2]
-        pooled, cot_half = conv(
+        pooled, cotangent_all = conv(
             nseq,
             nbatch,
             features[0],
@@ -553,7 +548,7 @@
             strided_weight.reshape(2 * width, -1),
             cotangent[0],
         )
-        layer_out, attended, cotangent_all = attention(
+        layer_out, attended = attention(
             nseq,
             nbatch,
             pooled,
@@ -565,7 +560,6 @@
             position_bias[0],
             interval_start,
             interval_end,
-            cot_half,
         )
         output_grad = lax.dot_general(
             attended,

time: 67.3 us -> 66.3 us (0.985)
  no operation moved by 1% of the time
where the time goes in v4:
time: 66.3 us; the launch traced here: 66.2 us
  Pallas kernels  60.1 us (91%)
  matrix products  4.75 us (7%)
  between operations  0.67 us (1%)
    pallas_call x1, Pallas kernels, conv(): pl.pallas_call(functools.partial(conv_kernel, nseq, nbatch), out_shape=(j...  31.7 us
    pallas_call x1, Pallas kernels, attention(): pl.pallas_call(functools.partial(attention_kernel, nseq, nbatch), out_sha...  28.4 us
    dot_general x1, matrix products, shards(): lax.dot_general(attended, cotangent_all, (((0,), (0,)), ((), ())), prefer...  4.75 us

profile of v4, /device:TPU:0, one launch (start us, length us, event | category | flops | bytes accessed | tf_op | source)
XLA Modules:
  0.0 66.2 jit_solution(16571852729290602616)
XLA Ops:
  0.6 31.7 %shard_map.131 = (bf16[16,1536]{1,0:T(8,128)(2,1)}, bf16[512,1536]{1,0:T(8,128)(2,1)}) custom-call(bf16[4096,768]{1,0:T(8,128)(2,1)} %bitcast.10, bf16[2304,384]{1,0:T(8,128)(2,1)} %bitcast.12, bf16[1536,768]{1,0:T(8,128)(2,1)} %bitcast.11, bf16[32,1536]{1,0:T(8,128)(2,1)} %bitcast.13), custom_call_target="tpu_custom_call" | custom-call | flops 12000000000 | bytes 8000000 | tf_op jit(solution)/shard_map/pallas_call | solution.py:286
  32.3 0.0 copy-start
  32.3 28.4 %shard_map.132 = (bf16[32,768]{1,0:T(8,128)(2,1)}, bf16[512,768]{1,0:T(8,128)(2,1)}) custom-call(bf16[16,1536]{1,0:T(8,128)(2,1)} %get-tuple-element.6.pooled, f32[1536]{0:T(1024)} %gain.1, bf16[1536,512]{1,0:T(8,128)(2,1)} %query_w.1, bf16[1536,512]{1,0:T(8,128)(2,1)} %key_w.1, bf16[1536,768]{1,0:T(8,128)(2,1)} %value_w.1, bf16[768,1536]{1,0:T(8,128)(2,1)} %output_w.1, ...), custom_call_target="tpu_custom_call" | custom-call | flops 400000000 | bytes 9000000 | tf_op jit(solution)/shard_map/pallas_call | solution.py:492
  60.8 0.0 copy-done
  60.8 0.0 copy-start.1
  60.8 4.7 %fusion = f32[768,1536]{1,0:T(8,128)} fusion(bf16[512,768]{1,0:T(8,128)(2,1)} %get-tuple-element.8, bf16[512,1536]{1,0:T(8,128)(2,1)S(1)} %copy-done), kind=kOutput, calls=%fused_computation | convolution fusion | flops 1207959552 | bytes 7077888 | tf_op jit(solution)/shard_map/dot_general | solution.py:564
  65.5 0.0 copy-done.1
  65.5 0.6 copy.15
Async XLA Ops:
  32.3 28.4 %copy-start = (bf16[512,1536]{1,0:T(8,128)(2,1)S(1)}, bf16[512,1536]{1,0:T(8,128)(2,1)}, u32[]{:S(2)}) copy-start(bf16[512,1536]{1,0:T(8,128)(2,1)} %get-tuple-element.9) | copy-start | bytes 4718596
  60.8 4.8 %copy-start.1 = (bf16[32,768]{1,0:T(8,128)(2,1)S(1)}, bf16[32,768]{1,0:T(8,128)(2,1)}, u32[]{:S(2)}) copy-start(bf16[32,768]{1,0:T(8,128)(2,1)} %get-tuple-element.7) | copy-start | bytes 147460

commit v5 on v4

--- a/solution.py
+++ b/solution.py
@@ -359,9 +359,6 @@
             ((key_w, wk), (value_w, wv), (query_w, wq), (output_w, wo))
         )
     ]
-    for load in loads:
-        load.start()
-
     enter(nseq, nbatch)
 
     mine = pl.ds(pl.multiple_of(c * half_rows, EDGE), half_rows)
@@ -375,6 +372,8 @@
         device_id_type=MESH,
     )
     swap.start()
+    for load in loads:
+        load.start()
     swap.wait()
 
     values = pool2[...].astype(jnp.float32)
@@ -475,8 +474,8 @@
         device_id_type=MESH,
     )
     swap_out.start()
+    own = jnp.dot(attended, wo[:, own_cols], preferred_element_type=jnp.float32)
     gather.forward()
-    own = jnp.dot(attended, wo[:, own_cols], preferred_element_type=jnp.float32)
     swap_out.wait()
     layer_out[...] = (proj[:, own_cols] + (own + other[1])).astype(jnp.bfloat16)
     gather.finish()

time: 66.3 us -> 65 us (0.980)
  Pallas kernels: 60.1 us -> 58.8 us
    pallas_call x1, Pallas kernels: 28.4 us -> 27.1 us  [attention(): pl.pallas_call(functools.partial(attention_kernel, nseq, nbatch), out_sha...]
where the time goes in v5:
time: 65 us; the launch traced here: 64.8 us
  Pallas kernels  58.8 us (90%)
  matrix products  4.75 us (7%)
  between operations  0.67 us (1%)
    pallas_call x1, Pallas kernels, conv(): pl.pallas_call(functools.partial(conv_kernel, nseq, nbatch), out_shape=(j...  31.7 us
    pallas_call x1, Pallas kernels, attention(): pl.pallas_call(functools.partial(attention_kernel, nseq, nbatch), out_sha...  27.1 us
    dot_general x1, matrix products, shards(): lax.dot_general(attended, cotangent_all, (((0,), (0,)), ((), ())), prefer...  4.75 us

profile of v5, /device:TPU:0, one launch (start us, length us, event | category | flops | bytes accessed | tf_op | source)
XLA Modules:
  0.0 64.8 jit_solution(13668718780720039107)
XLA Ops:
  0.6 31.7 %shard_map.131 = (bf16[16,1536]{1,0:T(8,128)(2,1)}, bf16[512,1536]{1,0:T(8,128)(2,1)}) custom-call(bf16[4096,768]{1,0:T(8,128)(2,1)} %bitcast.10, bf16[2304,384]{1,0:T(8,128)(2,1)} %bitcast.12, bf16[1536,768]{1,0:T(8,128)(2,1)} %bitcast.11, bf16[32,1536]{1,0:T(8,128)(2,1)} %bitcast.13), custom_call_target="tpu_custom_call" | custom-call | flops 12000000000 | bytes 8000000 | tf_op jit(solution)/shard_map/pallas_call | solution.py:286
  32.3 0.0 copy-start
  32.3 27.1 %shard_map.132 = (bf16[32,768]{1,0:T(8,128)(2,1)}, bf16[512,768]{1,0:T(8,128)(2,1)}) custom-call(bf16[16,1536]{1,0:T(8,128)(2,1)} %get-tuple-element.6.pooled, f32[1536]{0:T(1024)} %gain.1, bf16[1536,512]{1,0:T(8,128)(2,1)} %query_w.1, bf16[1536,512]{1,0:T(8,128)(2,1)} %key_w.1, bf16[1536,768]{1,0:T(8,128)(2,1)} %value_w.1, bf16[768,1536]{1,0:T(8,128)(2,1)} %output_w.1, ...), custom_call_target="tpu_custom_call" | custom-call | flops 400000000 | bytes 9000000 | tf_op jit(solution)/shard_map/pallas_call | solution.py:491
  59.4 0.0 copy-done
  59.4 0.0 copy-start.1
  59.4 4.7 %fusion = f32[768,1536]{1,0:T(8,128)} fusion(bf16[512,768]{1,0:T(8,128)(2,1)} %get-tuple-element.8, bf16[512,1536]{1,0:T(8,128)(2,1)S(1)} %copy-done), kind=kOutput, calls=%fused_computation | convolution fusion | flops 1207959552 | bytes 7077888 | tf_op jit(solution)/shard_map/dot_general | solution.py:563
  64.2 0.0 copy-done.1
  64.2 0.6 copy.15
Async XLA Ops:
  32.3 27.1 %copy-start = (bf16[512,1536]{1,0:T(8,128)(2,1)S(1)}, bf16[512,1536]{1,0:T(8,128)(2,1)}, u32[]{:S(2)}) copy-start(bf16[512,1536]{1,0:T(8,128)(2,1)} %get-tuple-element.9) | copy-start | bytes 4718596
  59.4 4.8 %copy-start.1 = (bf16[32,768]{1,0:T(8,128)(2,1)S(1)}, bf16[32,768]{1,0:T(8,128)(2,1)}, u32[]{:S(2)}) copy-start(bf16[32,768]{1,0:T(8,128)(2,1)} %get-tuple-element.7) | copy-start | bytes 147460
